TPU v7x, 32 devices: a whole 2x2x4 slice. The times are simulated.
32 devices in a mesh: rep: 2 (over x), seq: 16 (over z, y, core).
Axes of the slice: x: 2, y: 2, z: 4, core: 2. Of those that a mesh axis runs over, the one named last changes fastest.
Arguments:
- prompt_latent: bfloat16 [32, 2048, 512], P(('rep', 'seq')), parts along dimension 0, may hold values from -6 to 6
- prompt_rope: bfloat16 [32, 64, 2048], P(('rep', 'seq')), parts along dimension 0, may hold values from -8 to 8
- private_latent: bfloat16 [512, 128, 512], P(('rep', 'seq')), parts along dimension 0, may hold values from -6 to 6
- private_rope: bfloat16 [512, 64, 128], P(('rep', 'seq')), parts along dimension 0, may hold values from -6 to 6
- lengths: int32 [512], P(('rep', 'seq')), parts along dimension 0, may hold values from 1 to 128
- survived: int32 [512], P(('rep', 'seq')), parts along dimension 0, may hold values from 0 to 1
- prompt_of: int32 [512], P(('rep', 'seq')), parts along dimension 0, may hold values from 0 to 15, as said below
- new_slot: int32 [512], P(('rep', 'seq')), parts along dimension 0, may hold values from -1 to 255, as said below
- queries: bfloat16 [512, 2, 64, 576], P(('rep', 'seq')), parts along dimension 0, may hold values from -160 to 160
- new_keys: bfloat16 [512, 2, 576], P(('rep', 'seq')), parts along dimension 0, may hold values from -9 to 9
Outputs:
- attention: bfloat16 [512, 2, 64, 512], P(('rep', 'seq')), parts along dimension 0
There are 2 independent parts, one for each index of `rep`. A program takes and returns all parts, laid end to end along the dimension named above; each array names one. Nothing has to cross between parts.
Inputs may be any that keep to these rules, and one draw needn't show every extreme that they name: `prompt_of`: continuation rows d * 16 to (d + 1) * 16 - 1 belong to prompt d or prompt d - 1 (cyclically over the 16 prompts), 8 to each, so every prompt has 16 continuations. -1 exactly where survived is 0; distinct for distinct survivors; the slot's device new_slot // 16 lies within 2 devices of the continuation's own device (c // 16), cyclically; at most 2 survivors of one device go to any one other device, and some device sends exactly 2 to each device within 2.
All inputs are finite; a program needn't handle non-finite values.
Results may differ from a plain program's by a relative error of at most 0.0034.
Values may be sent and summed in bfloat16 or wider, within the bound.
A program may use at most 128 MiB of HBM per device.

v0:
```python
import jax
import jax.numpy as jnp
from jax import lax
from jax.sharding import PartitionSpec as P

DR = 64
NOPE = 128
REACH = 2
TRANSFER_LIMIT = 2


slot_pack = 4


def passed_along(block, axis, distance):
    devices = range(lax.axis_size(axis))
    route = [((i - distance) % len(devices), i) for i in devices]
    return lax.ppermute(block, axis, route)


def attend_pack(
    queries, new_keys, prompt_latent, prompt_rope, private_latent, private_rope, length
):
    pack, step_count, head_count, full_width = queries.shape
    lat_width = prompt_latent.shape[1]
    prompt_len = prompt_latent.shape[0]
    block_len = private_latent.shape[1]
    rows_per = step_count * head_count
    factor = (NOPE + DR) ** (-0.5)
    query_rows = queries.reshape(pack, rows_per, full_width)
    flat = query_rows.reshape(pack * rows_per, full_width)
    shared = lax.dot_general(
        flat[:, :lat_width],
        prompt_latent,
        (((1,), (1,)), ((), ())),
        preferred_element_type=jnp.float32,
    )
    shared = shared + jnp.dot(flat[:, lat_width:], prompt_rope, preferred_element_type=jnp.float32)
    shared = (shared * factor).reshape(pack, rows_per, prompt_len)
    batch_dims = (((2,), (2,)), ((0,), (0,)))
    inner = lax.dot_general(
        query_rows[:, :, :lat_width], private_latent, batch_dims, preferred_element_type=jnp.float32
    )
    inner = inner + lax.dot_general(
        query_rows[:, :, lat_width:],
        private_rope,
        (((2,), (1,)), ((0,), (0,))),
        preferred_element_type=jnp.float32,
    )
    inner = inner * factor
    fresh = lax.dot_general(
        query_rows[:, :, :lat_width],
        new_keys[:, :, :lat_width],
        batch_dims,
        preferred_element_type=jnp.float32,
    )
    fresh = fresh + lax.dot_general(
        query_rows[:, :, lat_width:],
        new_keys[:, :, lat_width:],
        batch_dims,
        preferred_element_type=jnp.float32,
    )
    fresh = fresh * factor
    inner_ok = jnp.arange(block_len, dtype=jnp.int32)[None, None, :] < length[:, None, None]
    step_of_row = jnp.arange(rows_per, dtype=jnp.int32) // head_count
    fresh_ok = jnp.arange(step_count, dtype=jnp.int32)[None, :] <= step_of_row[:, None]
    inner = jnp.where(inner_ok, inner, -1e30)
    fresh = jnp.where(fresh_ok[None, :, :], fresh, -1e30)
    row_top = jnp.maximum(
        jnp.max(shared, axis=2, keepdims=True),
        jnp.maximum(jnp.max(inner, axis=2, keepdims=True), jnp.max(fresh, axis=2, keepdims=True)),
    )
    shared_w = jnp.exp(shared - row_top)
    inner_w = jnp.exp(inner - row_top)
    fresh_w = jnp.exp(fresh - row_top)
    totals = (
        jnp.sum(shared_w, axis=2, keepdims=True)
        + jnp.sum(inner_w, axis=2, keepdims=True)
        + jnp.sum(fresh_w, axis=2, keepdims=True)
    )
    mixed = jnp.dot(
        shared_w.astype(jnp.bfloat16).reshape(pack * rows_per, prompt_len),
        prompt_latent,
        preferred_element_type=jnp.float32,
    ).reshape(pack, rows_per, lat_width)
    value_dims = (((2,), (1,)), ((0,), (0,)))
    mixed = mixed + lax.dot_general(
        inner_w.astype(jnp.bfloat16), private_latent, value_dims, preferred_element_type=jnp.float32
    )
    mixed = mixed + lax.dot_general(
        fresh_w.astype(jnp.bfloat16),
        new_keys[:, :, :lat_width],
        value_dims,
        preferred_element_type=jnp.float32,
    )
    mixed = mixed / totals
    return mixed.astype(jnp.bfloat16).reshape(pack, step_count, head_count, lat_width)


def signed_gap(target, my_index, processor_count):
    forward = (target - my_index) % processor_count
    return jnp.where(forward > processor_count // 2, forward - processor_count, forward)


def first_rows(marked, wanted_count):
    running = jnp.cumsum(marked.astype(jnp.int32)) - 1
    lane_ids = jnp.arange(wanted_count, dtype=jnp.int32)
    match_table = (running[None, :] == lane_ids[:, None]) & marked[None, :]
    is_found = jnp.any(match_table, axis=1)
    picked = jnp.sum(
        jnp.where(match_table, jnp.arange(marked.shape[0], dtype=jnp.int32)[None, :], 0), axis=1
    )
    return (picked, is_found)


def run_banks(has_job, job_bank, fetch_rows, banks_lat, banks_rot, out_shape):
    count = has_job.shape[0]
    result = jnp.zeros(out_shape, jnp.bfloat16)
    for bank_number in range(len(banks_lat)):
        marked = has_job & (job_bank == bank_number)
        picked, is_found = first_rows(marked, count)
        member_table = jnp.where(is_found, picked, -1).reshape(count // slot_pack, slot_pack)
        group_count = (jnp.sum(marked.astype(jnp.int32)) + slot_pack - 1) // slot_pack
        bank_lat = banks_lat[bank_number]
        bank_rot = banks_rot[bank_number]

        def advance(
            number, current, member_table=member_table, bank_lat=bank_lat, bank_rot=bank_rot
        ):
            rows = member_table[number]
            is_live = rows >= 0
            safe_rows = jnp.maximum(rows, 0)
            slot_parts = fetch_rows(safe_rows)
            output = attend_pack(
                slot_parts[0],
                slot_parts[1],
                bank_lat,
                bank_rot,
                slot_parts[2],
                slot_parts[3],
                slot_parts[4],
            )
            return current.at[jnp.where(is_live, rows, count)].set(output, mode="drop")

        result = lax.fori_loop(0, group_count, advance, result)
    return result


def per_device(
    prompt_latent,
    prompt_rope,
    private_latent,
    private_rope,
    lengths,
    survived,
    prompt_of,
    new_slot,
    queries,
    new_keys,
):
    processor_count = lax.axis_size("seq")
    my_index = lax.axis_index("seq")
    members = lengths.shape[0]
    alive_mask = survived > 0
    target_dev = jnp.where(alive_mask, new_slot // members, my_index)
    target_pos = jnp.where(alive_mask, new_slot % members, 0)
    offset = jnp.where(
        alive_mask, signed_gap(target_dev, my_index, processor_count), processor_count
    )
    from_prior = (prompt_of != my_index).astype(jnp.int32)
    prior_latent, prior_rope = passed_along((prompt_latent, prompt_rope), "seq", 1)
    offsets = [amount for amount in range(-REACH, REACH + 1) if amount != 0]
    out_shape = (members,) + queries.shape[1:3] + (prompt_latent.shape[2],)
    member_ids = jnp.arange(TRANSFER_LIMIT, dtype=jnp.int32)
    query_bank = [queries]
    key_bank = [new_keys]
    claim_lists = []
    pick_lists = []
    bank_pos = jnp.where(offset == 0, target_pos, 0)
    for lane_number, shift_by in enumerate(offsets):
        picked, is_found = first_rows(offset == shift_by, TRANSFER_LIMIT)
        wanted = jnp.where(is_found, target_pos[picked], -1)
        claimed = passed_along(wanted, "seq", shift_by)
        rows_needed = jnp.maximum(claimed, 0)
        back_query, back_keys = passed_along(
            (queries[rows_needed], new_keys[rows_needed]), "seq", -shift_by
        )
        query_bank.append(back_query)
        key_bank.append(back_keys)
        bank_spot = members + lane_number * TRANSFER_LIMIT + member_ids
        bank_pos = bank_pos.at[jnp.where(is_found, picked, members)].set(bank_spot, mode="drop")
        claim_lists.append(claimed)
        pick_lists.append(picked)
    all_query = jnp.concatenate(query_bank, axis=0)
    all_keys = jnp.concatenate(key_bank, axis=0)

    def fetch_home(cont_rows):
        spots = bank_pos[cont_rows]
        return (
            all_query[spots],
            all_keys[spots],
            private_latent[cont_rows],
            private_rope[cont_rows],
            lengths[cont_rows],
        )

    results = run_banks(
        alive_mask,
        from_prior,
        fetch_home,
        [prompt_latent[0], prior_latent[0]],
        [prompt_rope[0], prior_rope[0]],
        out_shape,
    )
    final = (
        jnp.zeros(out_shape, jnp.bfloat16)
        .at[jnp.where(offset == 0, target_pos, members)]
        .set(results, mode="drop")
    )
    for lane_number, shift_by in enumerate(offsets):
        arrived = passed_along(results[pick_lists[lane_number]], "seq", shift_by)
        claimed = claim_lists[lane_number]
        final = final.at[jnp.where(claimed >= 0, claimed, members)].set(arrived, mode="drop")
    return final


def solution(mesh):
    return jax.shard_map(
        per_device,
        mesh=mesh,
        in_specs=(
            P(("rep", "seq"), None, None),
            P(("rep", "seq"), None, None),
            P(("rep", "seq"), None, None),
            P(("rep", "seq"), None, None),
            P(("rep", "seq")),
            P(("rep", "seq")),
            P(("rep", "seq")),
            P(("rep", "seq")),
            P(("rep", "seq"), None, None, None),
            P(("rep", "seq"), None, None),
        ),
        out_specs=P(("rep", "seq"), None, None, None),
        check_vma=False,
    )
```

profile of v0, /device:TPU:1, one launch (start us, length us, event | category | flops | bytes accessed | tf_op | source)
XLA Modules:
  0.0 207.8 jit_solution(17348570470961812321)
XLA Ops:
  1.7 1.3 compare_select_fusion.29
  3.7 5.1 %collective-permute-start = (s32[2]{0:T(128)S(1)}, s32[2]{0:T(128)S(1)}, u32[]{:S(2)}, u32[]{:S(2)}) collective-permute-start(s32[2]{0:T(128)S(1)} %broadcast_select_fusion.3), channel_id=1, source_target_pairs={{2,0},{3,1},{4,2},{5,3},{6,4},{7,5},{8,6},{9,7},{10,8},{11,9},{12,... | collective-permute-start | bytes 32 | tf_op jit(solution)/shard_map/ppermute | solution.py:18
  16.3 3.6 %constant_dynamic-update-slice_fusion.4 = bf16[24,2,64,576]{3,2,1,0:T(8,128)(2,1)} fusion(bf16[16,2,64,576]{3,2,1,0:T(8,128)(2,1)} %param.22), kind=kLoop, calls=%fused_computation.155 | loop fusion | bytes 4980736
  35.2 13.3 %collective-permute-done.8 = bf16[2,2,576]{2,1,0:T(2,128)(2,1)S(1)} collective-permute-done((bf16[2,2,576]{2,1,0:T(2,128)(2,1)S(1)}, bf16[2,2,576]{2,1,0:T(2,128)(2,1)S(1)}, u32[]{:S(2)}, u32[]{:S(2)}) %collective-permute-start.8) | collective-permute-done | bytes 4640 | tf_op jit(solution)/shard_map/ppermute | solution.py:18
  49.0 1.4 collective-permute-done.9
  50.4 5.5 %collective-permute-start.10 = (bf16[2,2,576]{2,1,0:T(2,128)(2,1)S(1)}, bf16[2,2,576]{2,1,0:T(2,128)(2,1)S(1)}, u32[]{:S(2)}, u32[]{:S(2)}) collective-permute-start(bf16[2,2,576]{2,1,0:T(2,128)(2,1)S(1)} %gather_fusion.22), channel_id=1, source_target_pairs={{1,0},{2,1},{3,2},{4,3},{5,4},{6,5},{7,6},{8,7},{9,8},{10,9},{11,1... | collective-permute-start | bytes 13832 | tf_op jit(solution)/shard_map/ppermute | solution.py:18
  56.7 4.5 %collective-permute-start.11 = (bf16[2,2,576]{2,1,0:T(2,128)(2,1)S(1)}, bf16[2,2,576]{2,1,0:T(2,128)(2,1)S(1)}, u32[]{:S(2)}, u32[]{:S(2)}) collective-permute-start(bf16[2,2,576]{2,1,0:T(2,128)(2,1)S(1)} %gather_fusion.23), channel_id=1, source_target_pairs={{2,0},{3,1},{4,2},{5,3},{6,4},{7,5},{8,6},{9,7},{10,8},{11,9},{12,... | collective-permute-start | bytes 13832 | tf_op jit(solution)/shard_map/ppermute | solution.py:18
  62.6 4.4 %collective-permute-start.7 = (bf16[2,2,64,576]{3,2,1,0:T(8,128)(2,1)S(1)}, bf16[2,2,64,576]{3,2,1,0:T(8,128)(2,1)S(1)}, u32[]{:S(2)}, u32[]{:S(2)}) collective-permute-start(bf16[2,2,64,576]{3,2,1,0:T(8,128)(2,1)S(1)} %gather_fusion.19), channel_id=1, source_target_pairs={{2,0},{3,1},{4,2},{5,3},{6,4},{7,5},{8,6},{9,7},{10,8},{11,9},{12,... | collective-permute-start | bytes 884744 | tf_op jit(solution)/shard_map/ppermute | solution.py:18
  68.5 3.5 %collective-permute-done.5 = bf16[2,2,64,576]{3,2,1,0:T(8,128)(2,1)S(1)} collective-permute-done((bf16[2,2,64,576]{3,2,1,0:T(8,128)(2,1)S(1)}, bf16[2,2,64,576]{3,2,1,0:T(8,128)(2,1)S(1)}, u32[]{:S(2)}, u32[]{:S(2)}) %collective-permute-start.5) | collective-permute-done | bytes 294944 | tf_op jit(solution)/shard_map/ppermute | solution.py:18
  72.8 1.8 collective-permute-done.7
  75.5 51.6 %while.24 = (s32[]{:T(128)}, bf16[16,2,64,512]{3,2,1,0:T(8,128)(2,1)S(1)}, s32[]{:T(128)}, s32[4,4]{1,0:T(4,128)S(1)}, s32[16]{0:T(128)S(1)}, /*index=5*/bf16[24...) while((s32[]{:T(128)}, ...), condition=%wide.region_28.29_spmd, body=%wide.region_20.28_spmd.sunk | while | flops 2434412288 | bytes 38641580 | solution.py:145
  76.9 2.8 %gather_fusion.1 = bf16[4,2,64,576]{3,2,1,0:T(8,128)(2,1)S(1)} fusion(bf16[24,2,64,576]{3,2,1,0:T(8,128)(2,1)} %get-tuple-element.648, s32[1024]{0:T(1024)S(1)} %pad_clamp_fusion.17), kind=kCustom, calls=%fused_computation.1.clone.1 | custom fusion | bytes 1179664 | tf_op jit(solution)/shard_map/while/body/gather | solution.py:200
  79.6 2.2 %gather_fusion.2 = bf16[4,128,512]{2,1,0:T(8,128)(2,1)S(1)} fusion(bf16[16,128,512]{2,1,0:T(8,128)(2,1)} %get-tuple-element.652, s32[1024]{0:T(1024)S(1)} %pad_clamp_fusion.16), kind=kCustom, calls=%fused_computation.3.clone.1 | custom fusion | bytes 1048592 | tf_op jit(solution)/shard_map/while/body/gather | solution.py:202
  82.8 2.1 %gather_fusion.3 = bf16[4,64,128]{2,1,0:T(8,128)(2,1)} fusion(bf16[16,64,128]{2,1,0:T(8,128)(2,1)} %get-tuple-element.653, s32[1024]{0:T(1024)S(1)} %pad_clamp_fusion.16), kind=kCustom, calls=%fused_computation.4.clone.1 | custom fusion | bytes 131088 | tf_op jit(solution)/shard_map/while/body/gather | solution.py:203
  86.9 2.1 %gather_fusion.5 = bf16[4,2,576]{2,1,0:T(2,128)(2,1)} fusion(bf16[24,2,576]{2,1,0:T(2,128)(2,1)} %get-tuple-element.654, s32[1024]{0:T(1024)} %copy-done.4), kind=kCustom, calls=%fused_computation.5.clone.1 | custom fusion | bytes 18448 | tf_op jit(solution)/shard_map/while/body/gather | solution.py:201
  90.9 2.9 %fusion.179 = f32[512,2048]{1,0:T(8,128)S(1)} fusion(bf16[2048,512]{1,0:T(8,128)(2,1)} %get-tuple-element.649, bf16[512,576]{1,0:T(8,128)(2,1)S(1)} %bitcast.220), kind=kOutput, calls=%fused_computation.55.clone.1 | convolution fusion | flops 1073741824 | bytes 6815744 | tf_op jit(solution)/shard_map/while/body/dot_general | solution.py:32
  93.8 1.7 fusion.180
  96.4 2.8 %fusion.186 = f32[4,128,512]{2,1,0:T(8,128)S(1)} fusion(bf16[4,128,2048]{2,1,0:T(8,128)(2,1)S(1)} %bitcast.228, bf16[2048,512]{1,0:T(8,128)(2,1)} %get-tuple-element.649), kind=kOutput, calls=%fused_computation.43.clone.1 | convolution fusion | flops 1073741824 | bytes 5242880 | tf_op jit(solution)/shard_map/while/body/dot_general | solution.py:81
  102.7 2.8 %gather_fusion.1 = bf16[4,2,64,576]{3,2,1,0:T(8,128)(2,1)S(1)} fusion(bf16[24,2,64,576]{3,2,1,0:T(8,128)(2,1)} %get-tuple-element.648, s32[1024]{0:T(1024)S(1)} %pad_clamp_fusion.17), kind=kCustom, calls=%fused_computation.1.clone.1 | custom fusion | bytes 1179664 | tf_op jit(solution)/shard_map/while/body/gather | solution.py:200
  105.4 2.2 %gather_fusion.2 = bf16[4,128,512]{2,1,0:T(8,128)(2,1)S(1)} fusion(bf16[16,128,512]{2,1,0:T(8,128)(2,1)} %get-tuple-element.652, s32[1024]{0:T(1024)S(1)} %pad_clamp_fusion.16), kind=kCustom, calls=%fused_computation.3.clone.1 | custom fusion | bytes 1048592 | tf_op jit(solution)/shard_map/while/body/gather | solution.py:202
  108.6 2.1 %gather_fusion.3 = bf16[4,64,128]{2,1,0:T(8,128)(2,1)} fusion(bf16[16,64,128]{2,1,0:T(8,128)(2,1)} %get-tuple-element.653, s32[1024]{0:T(1024)S(1)} %pad_clamp_fusion.16), kind=kCustom, calls=%fused_computation.4.clone.1 | custom fusion | bytes 131088 | tf_op jit(solution)/shard_map/while/body/gather | solution.py:203
  112.7 2.1 %gather_fusion.5 = bf16[4,2,576]{2,1,0:T(2,128)(2,1)} fusion(bf16[24,2,576]{2,1,0:T(2,128)(2,1)} %get-tuple-element.654, s32[1024]{0:T(1024)} %copy-done.4), kind=kCustom, calls=%fused_computation.5.clone.1 | custom fusion | bytes 18448 | tf_op jit(solution)/shard_map/while/body/gather | solution.py:201
  116.7 2.9 %fusion.179 = f32[512,2048]{1,0:T(8,128)S(1)} fusion(bf16[2048,512]{1,0:T(8,128)(2,1)} %get-tuple-element.649, bf16[512,576]{1,0:T(8,128)(2,1)S(1)} %bitcast.220), kind=kOutput, calls=%fused_computation.55.clone.1 | convolution fusion | flops 1073741824 | bytes 6815744 | tf_op jit(solution)/shard_map/while/body/dot_general | solution.py:32
  119.6 1.7 fusion.180
  122.2 2.8 %fusion.186 = f32[4,128,512]{2,1,0:T(8,128)S(1)} fusion(bf16[4,128,2048]{2,1,0:T(8,128)(2,1)S(1)} %bitcast.228, bf16[2048,512]{1,0:T(8,128)(2,1)} %get-tuple-element.649), kind=kOutput, calls=%fused_computation.43.clone.1 | convolution fusion | flops 1073741824 | bytes 5242880 | tf_op jit(solution)/shard_map/while/body/dot_general | solution.py:81
  127.2 52.9 %while.25 = (s32[]{:T(128)}, bf16[16,2,64,512]{3,2,1,0:T(8,128)(2,1)S(1)}, s32[]{:T(128)}, s32[4,4]{1,0:T(4,128)}, s32[16]{0:T(128)S(1)}, /*index=5*/bf16[24,2,6...) while((s32[]{:T(128)}, ...), condition=%wide.region_41.42_spmd, body=%wide.region_33.41_spmd.sunk | while | flops 2434412288 | bytes 38641012 | solution.py:145
  129.3 2.8 %gather_fusion.7 = bf16[4,2,64,576]{3,2,1,0:T(8,128)(2,1)S(1)} fusion(bf16[24,2,64,576]{3,2,1,0:T(8,128)(2,1)} %get-tuple-element.693, s32[1024]{0:T(1024)S(1)} %pad_clamp_fusion.19), kind=kCustom, calls=%fused_computation.7.clone.1 | custom fusion | bytes 1179664 | tf_op jit(solution)/shard_map/while/body/gather | solution.py:200
  132.1 2.2 %gather_fusion.8 = bf16[4,128,512]{2,1,0:T(8,128)(2,1)S(1)} fusion(bf16[16,128,512]{2,1,0:T(8,128)(2,1)} %get-tuple-element.697, s32[1024]{0:T(1024)S(1)} %pad_clamp_fusion.18), kind=kCustom, calls=%fused_computation.9.clone.1 | custom fusion | bytes 1048592 | tf_op jit(solution)/shard_map/while/body/gather | solution.py:202
  135.2 2.1 %gather_fusion.9 = bf16[4,64,128]{2,1,0:T(8,128)(2,1)} fusion(bf16[16,64,128]{2,1,0:T(8,128)(2,1)} %get-tuple-element.698, s32[1024]{0:T(1024)S(1)} %pad_clamp_fusion.18), kind=kCustom, calls=%fused_computation.10.clone.1 | custom fusion | bytes 131088 | tf_op jit(solution)/shard_map/while/body/gather | solution.py:203
  139.3 2.1 %gather_fusion.11 = bf16[4,2,576]{2,1,0:T(2,128)(2,1)} fusion(bf16[24,2,576]{2,1,0:T(2,128)(2,1)} %get-tuple-element.699, s32[1024]{0:T(1024)} %copy-done.5), kind=kCustom, calls=%fused_computation.11.clone.1 | custom fusion | bytes 18448 | tf_op jit(solution)/shard_map/while/body/gather | solution.py:201
  143.3 2.9 %fusion.207 = f32[512,2048]{1,0:T(8,128)S(1)} fusion(bf16[2048,512]{1,0:T(8,128)(2,1)} %get-tuple-element.694, bf16[512,576]{1,0:T(8,128)(2,1)S(1)} %bitcast.226), kind=kOutput, calls=%fused_computation.111.clone.1 | convolution fusion | flops 1073741824 | bytes 6815744 | tf_op jit(solution)/shard_map/while/body/dot_general | solution.py:32
  146.2 1.7 fusion.208
  148.8 2.8 %fusion.214 = f32[4,128,512]{2,1,0:T(8,128)S(1)} fusion(bf16[4,128,2048]{2,1,0:T(8,128)(2,1)S(1)} %bitcast.229, bf16[2048,512]{1,0:T(8,128)(2,1)} %get-tuple-element.694), kind=kOutput, calls=%fused_computation.99.clone.1 | convolution fusion | flops 1073741824 | bytes 5242880 | tf_op jit(solution)/shard_map/while/body/dot_general | solution.py:81
  155.6 2.8 %gather_fusion.7 = bf16[4,2,64,576]{3,2,1,0:T(8,128)(2,1)S(1)} fusion(bf16[24,2,64,576]{3,2,1,0:T(8,128)(2,1)} %get-tuple-element.693, s32[1024]{0:T(1024)S(1)} %pad_clamp_fusion.19), kind=kCustom, calls=%fused_computation.7.clone.1 | custom fusion | bytes 1179664 | tf_op jit(solution)/shard_map/while/body/gather | solution.py:200
  158.4 2.2 %gather_fusion.8 = bf16[4,128,512]{2,1,0:T(8,128)(2,1)S(1)} fusion(bf16[16,128,512]{2,1,0:T(8,128)(2,1)} %get-tuple-element.697, s32[1024]{0:T(1024)S(1)} %pad_clamp_fusion.18), kind=kCustom, calls=%fused_computation.9.clone.1 | custom fusion | bytes 1048592 | tf_op jit(solution)/shard_map/while/body/gather | solution.py:202
  161.6 2.1 %gather_fusion.9 = bf16[4,64,128]{2,1,0:T(8,128)(2,1)} fusion(bf16[16,64,128]{2,1,0:T(8,128)(2,1)} %get-tuple-element.698, s32[1024]{0:T(1024)S(1)} %pad_clamp_fusion.18), kind=kCustom, calls=%fused_computation.10.clone.1 | custom fusion | bytes 131088 | tf_op jit(solution)/shard_map/while/body/gather | solution.py:203
  165.7 2.1 %gather_fusion.11 = bf16[4,2,576]{2,1,0:T(2,128)(2,1)} fusion(bf16[24,2,576]{2,1,0:T(2,128)(2,1)} %get-tuple-element.699, s32[1024]{0:T(1024)} %copy-done.5), kind=kCustom, calls=%fused_computation.11.clone.1 | custom fusion | bytes 18448 | tf_op jit(solution)/shard_map/while/body/gather | solution.py:201
  169.6 2.9 %fusion.207 = f32[512,2048]{1,0:T(8,128)S(1)} fusion(bf16[2048,512]{1,0:T(8,128)(2,1)} %get-tuple-element.694, bf16[512,576]{1,0:T(8,128)(2,1)S(1)} %bitcast.226), kind=kOutput, calls=%fused_computation.111.clone.1 | convolution fusion | flops 1073741824 | bytes 6815744 | tf_op jit(solution)/shard_map/while/body/dot_general | solution.py:32
  172.5 1.7 fusion.208
  175.2 2.8 %fusion.214 = f32[4,128,512]{2,1,0:T(8,128)S(1)} fusion(bf16[4,128,2048]{2,1,0:T(8,128)(2,1)S(1)} %bitcast.229, bf16[2048,512]{1,0:T(8,128)(2,1)} %get-tuple-element.694), kind=kOutput, calls=%fused_computation.99.clone.1 | convolution fusion | flops 1073741824 | bytes 5242880 | tf_op jit(solution)/shard_map/while/body/dot_general | solution.py:81
  180.8 5.4 %collective-permute-start.14 = (bf16[2,2,64,512]{3,2,1,0:T(8,128)(2,1)S(1)}, bf16[2,2,64,512]{3,2,1,0:T(8,128)(2,1)}, u32[]{:S(2)}, u32[]{:S(2)}) collective-permute-start(bf16[2,2,64,512]{3,2,1,0:T(8,128)(2,1)S(1)} %gather_fusion.24), channel_id=1, source_target_pairs={{2,0},{3,1},{4,2},{5,3},{6,4},{7,5},{8,6},{9,7},{10,8},{11,9},{12,... | collective-permute-start | bytes 786440 | tf_op jit(solution)/shard_map/ppermute | solution.py:18
  186.8 3.8 %collective-permute-start.15 = (bf16[2,2,64,512]{3,2,1,0:T(8,128)(2,1)S(1)}, bf16[2,2,64,512]{3,2,1,0:T(8,128)(2,1)}, u32[]{:S(2)}, u32[]{:S(2)}) collective-permute-start(bf16[2,2,64,512]{3,2,1,0:T(8,128)(2,1)S(1)} %gather_fusion.25), channel_id=1, source_target_pairs={{1,0},{2,1},{3,2},{4,3},{5,4},{6,5},{7,6},{8,7},{9,8},{10,9},{11,1... | collective-permute-start | bytes 786440 | tf_op jit(solution)/shard_map/ppermute | solution.py:18
  192.2 1.6 broadcast.604
  193.7 4.8 %scatter_fusion.6 = bf16[16,2,64,512]{3,2,1,0:T(8,128)(2,1)} fusion(bf16[16,2,64,512]{3,2,1,0:T(8,128)(2,1)} %broadcast.604, s32[16]{0:T(128)S(1)} %compare_select_fusion.22, bf16[16,2,64,512]{3,2,1,0:T(8,128)(2,1)S(1)} %get-tuple-element.312), kind=kCustom, calls=%fused_computation.34 | custom fusion | bytes 6291520 | tf_op jit(solution)/shard_map/scatter | solution.py:218
  198.6 2.3 %scatter_fusion.7 = bf16[16,2,64,512]{3,2,1,0:T(8,128)(2,1)} fusion(bf16[16,2,64,512]{3,2,1,0:T(8,128)(2,1)} %scatter_fusion.6, s32[2]{0:T(128)S(1)} %copy-done.17, bf16[2,2,64,512]{3,2,1,0:T(8,128)(2,1)} %collective-permute-done.14), kind=kCustom, calls=%fused_computation.35 | custom fusion | bytes 786440 | tf_op jit(solution)/shard_map/scatter | solution.py:223
  200.9 2.3 %scatter_fusion.8 = bf16[16,2,64,512]{3,2,1,0:T(8,128)(2,1)} fusion(bf16[16,2,64,512]{3,2,1,0:T(8,128)(2,1)} %scatter_fusion.7, s32[2]{0:T(128)S(1)} %copy-done.18, bf16[2,2,64,512]{3,2,1,0:T(8,128)(2,1)} %collective-permute-done.15), kind=kCustom, calls=%fused_computation.36 | custom fusion | bytes 786440 | tf_op jit(solution)/shard_map/scatter | solution.py:223
  203.3 2.3 %scatter_fusion.9 = bf16[16,2,64,512]{3,2,1,0:T(8,128)(2,1)} fusion(bf16[16,2,64,512]{3,2,1,0:T(8,128)(2,1)} %scatter_fusion.8, s32[2]{0:T(128)S(1)} %copy-done.19, bf16[2,2,64,512]{3,2,1,0:T(8,128)(2,1)} %collective-permute-done.16), kind=kCustom, calls=%fused_computation.37 | custom fusion | bytes 786440 | tf_op jit(solution)/shard_map/scatter | solution.py:223
  205.6 2.2 %scatter_fusion.10 = bf16[16,2,64,512]{3,2,1,0:T(8,128)(2,1)} fusion(bf16[16,2,64,512]{3,2,1,0:T(8,128)(2,1)} %scatter_fusion.9, s32[2]{0:T(128)S(1)} %copy-done.20, bf16[2,2,64,512]{3,2,1,0:T(8,128)(2,1)S(1)} %collective-permute-done.17), kind=kCustom, calls=%fused_computation.38 | custom fusion | bytes 786440 | tf_op jit(solution)/shard_map/scatter | solution.py:223
  (260 shorter events, 69.6 us)
Async XLA Ops:
  0.7 9.7 %copy-start.15 = (s32[16]{0:T(128)}, s32[16]{0:T(128)S(1)}, u32[]{:S(2)}) copy-start(s32[16]{0:T(128)S(1)} %get-tuple-element.400) | copy-start | bytes 196
  3.0 7.4 %copy-start.11 = (s32[1024]{0:T(1024)}, s32[1024]{0:T(1024)S(1)}, u32[]{:S(2)}) copy-start(s32[1024]{0:T(1024)S(1)} %get-tuple-element.423) | copy-start | bytes 12292
  3.1 7.4 %copy-start.12 = (s32[1024]{0:T(1024)}, s32[1024]{0:T(1024)S(1)}, u32[]{:S(2)}) copy-start(s32[1024]{0:T(1024)S(1)} %get-tuple-element.424) | copy-start | bytes 12292
  3.7 19.9 %collective-permute-start = (s32[2]{0:T(128)S(1)}, s32[2]{0:T(128)S(1)}, u32[]{:S(2)}, u32[]{:S(2)}) collective-permute-start(s32[2]{0:T(128)S(1)} %broadcast_select_fusion.3), channel_id=1, source_target_pairs={{2,0},{3,1},{4,2},{5,3},{6,4},{7,5},{8,6},{9,7},{10,8},{11,9},{12,... | collective-permute-start | bytes 32 | tf_op jit(solution)/shard_map/ppermute | solution.py:18
  9.5 14.8 %collective-permute-start.2 = (s32[2]{0:T(128)S(1)}, s32[2]{0:T(128)S(1)}, u32[]{:S(2)}, u32[]{:S(2)}) collective-permute-start(s32[2]{0:T(128)S(1)} %broadcast_select_fusion.2), channel_id=1, source_target_pairs={{1,0},{2,1},{3,2},{4,3},{5,4},{6,5},{7,6},{8,7},{9,8},{10,9},{11,1... | collective-permute-start | bytes 32 | tf_op jit(solution)/shard_map/ppermute | solution.py:18
  11.4 3.5 %copy-start.13 = (s32[1024]{0:T(1024)}, s32[1024]{0:T(1024)S(1)}, u32[]{:S(2)}) copy-start(s32[1024]{0:T(1024)S(1)} %get-tuple-element.421) | copy-start | bytes 12292
  11.5 3.5 %copy-start.14 = (s32[1024]{0:T(1024)}, s32[1024]{0:T(1024)S(1)}, u32[]{:S(2)}) copy-start(s32[1024]{0:T(1024)S(1)} %get-tuple-element.422) | copy-start | bytes 12292
  12.1 12.8 %collective-permute-start.4 = (s32[2]{0:T(128)S(1)}, s32[2]{0:T(128)S(1)}, u32[]{:S(2)}, u32[]{:S(2)}) collective-permute-start(s32[2]{0:T(128)S(1)} %broadcast_select_fusion.1), channel_id=1, source_target_pairs={{15,0},{0,1},{1,2},{2,3},{3,4},{4,5},{5,6},{6,7},{7,8},{8,9},{9,10... | collective-permute-start | bytes 32 | tf_op jit(solution)/shard_map/ppermute | solution.py:18
  13.5 13.7 %collective-permute-start.6 = (s32[2]{0:T(128)S(1)}, s32[2]{0:T(128)S(1)}, u32[]{:S(2)}, u32[]{:S(2)}) collective-permute-start(s32[2]{0:T(128)S(1)} %broadcast_select_fusion), channel_id=1, source_target_pairs={{14,0},{15,1},{0,2},{1,3},{2,4},{3,5},{4,6},{5,7},{6,8},{7,9},{8,1... | collective-permute-start | bytes 32 | tf_op jit(solution)/shard_map/ppermute | solution.py:18
  13.6 113.6 %collective-permute-start.12 = (bf16[1,2048,512]{2,1,0:T(8,128)(2,1)}, bf16[1,2048,512]{2,1,0:T(8,128)(2,1)}, u32[]{:S(2)}, u32[]{:S(2)}) collective-permute-start(bf16[1,2048,512]{2,1,0:T(8,128)(2,1)} %param.14), channel_id=1, source_target_pairs={{15,0},{0,1},{1,2},{2,3},{3,4},{4,5},{5,6},{6,7},{7,8},{8,9},{9,10... | collective-permute-start | bytes 6291464 | tf_op jit(solution)/shard_map/ppermute | solution.py:18
  16.3 3.6 %copy-start.6 = (bf16[16,2,576]{2,1,0:T(2,128)(2,1)S(1)}, bf16[16,2,576]{2,1,0:T(2,128)(2,1)}, u32[]{:S(2)}) copy-start(bf16[16,2,576]{2,1,0:T(2,128)(2,1)} %param.23) | copy-start | bytes 110596
  21.3 6.5 %copy-start.1 = (bf16[16,2,64,576]{3,2,1,0:T(8,128)(2,1)S(1)}, bf16[16,2,64,576]{3,2,1,0:T(8,128)(2,1)}, u32[]{:S(2)}) copy-start(bf16[16,2,64,576]{3,2,1,0:T(8,128)(2,1)} %param.22) | copy-start | bytes 7077892
  23.7 103.5 %collective-permute-start.13 = (bf16[1,64,2048]{2,1,0:T(8,128)(2,1)}, bf16[1,64,2048]{2,1,0:T(8,128)(2,1)}, u32[]{:S(2)}, u32[]{:S(2)}) collective-permute-start(bf16[1,64,2048]{2,1,0:T(8,128)(2,1)} %param.15), channel_id=1, source_target_pairs={{15,0},{0,1},{1,2},{2,3},{3,4},{4,5},{5,6},{6,7},{7,8},{8,9},{9,10... | collective-permute-start | bytes 786440 | tf_op jit(solution)/shard_map/ppermute | solution.py:18
  26.0 22.4 %collective-permute-start.8 = (bf16[2,2,576]{2,1,0:T(2,128)(2,1)S(1)}, bf16[2,2,576]{2,1,0:T(2,128)(2,1)S(1)}, u32[]{:S(2)}, u32[]{:S(2)}) collective-permute-start(bf16[2,2,576]{2,1,0:T(2,128)(2,1)S(1)} %gather_fusion.20), channel_id=1, source_target_pairs={{14,0},{15,1},{0,2},{1,3},{2,4},{3,5},{4,6},{5,7},{6,8},{7,9},{8,1... | collective-permute-start | bytes 13832 | tf_op jit(solution)/shard_map/ppermute | solution.py:18
  33.4 29.2 %collective-permute-start.1 = (bf16[2,2,64,576]{3,2,1,0:T(8,128)(2,1)}, bf16[2,2,64,576]{3,2,1,0:T(8,128)(2,1)S(1)}, u32[]{:S(2)}, u32[]{:S(2)}) collective-permute-start(bf16[2,2,64,576]{3,2,1,0:T(8,128)(2,1)} %gather_fusion.13), channel_id=1, source_target_pairs={{14,0},{15,1},{0,2},{1,3},{2,4},{3,5},{4,6},{5,7},{6,8},{7,9},{8,1... | collective-permute-start | bytes 884744 | tf_op jit(solution)/shard_map/ppermute | solution.py:18
  34.3 33.5 %collective-permute-start.3 = (bf16[2,2,64,576]{3,2,1,0:T(8,128)(2,1)}, bf16[2,2,64,576]{3,2,1,0:T(8,128)(2,1)S(1)}, u32[]{:S(2)}, u32[]{:S(2)}) collective-permute-start(bf16[2,2,64,576]{3,2,1,0:T(8,128)(2,1)} %gather_fusion.15), channel_id=1, source_target_pairs={{15,0},{0,1},{1,2},{2,3},{3,4},{4,5},{5,6},{6,7},{7,8},{8,9},{9,10... | collective-permute-start | bytes 884744 | tf_op jit(solution)/shard_map/ppermute | solution.py:18
  48.4 2.0 collective-permute-start.9
  50.4 6.3 %collective-permute-start.10 = (bf16[2,2,576]{2,1,0:T(2,128)(2,1)S(1)}, bf16[2,2,576]{2,1,0:T(2,128)(2,1)S(1)}, u32[]{:S(2)}, u32[]{:S(2)}) collective-permute-start(bf16[2,2,576]{2,1,0:T(2,128)(2,1)S(1)} %gather_fusion.22), channel_id=1, source_target_pairs={{1,0},{2,1},{3,2},{4,3},{5,4},{6,5},{7,6},{8,7},{9,8},{10,9},{11,1... | collective-permute-start | bytes 13832 | tf_op jit(solution)/shard_map/ppermute | solution.py:18
  56.7 5.3 %collective-permute-start.11 = (bf16[2,2,576]{2,1,0:T(2,128)(2,1)S(1)}, bf16[2,2,576]{2,1,0:T(2,128)(2,1)S(1)}, u32[]{:S(2)}, u32[]{:S(2)}) collective-permute-start(bf16[2,2,576]{2,1,0:T(2,128)(2,1)S(1)} %gather_fusion.23), channel_id=1, source_target_pairs={{2,0},{3,1},{4,2},{5,3},{6,4},{7,5},{8,6},{9,7},{10,8},{11,9},{12,... | collective-permute-start | bytes 13832 | tf_op jit(solution)/shard_map/ppermute | solution.py:18
  62.0 10.0 %collective-permute-start.5 = (bf16[2,2,64,576]{3,2,1,0:T(8,128)(2,1)S(1)}, bf16[2,2,64,576]{3,2,1,0:T(8,128)(2,1)S(1)}, u32[]{:S(2)}, u32[]{:S(2)}) collective-permute-start(bf16[2,2,64,576]{3,2,1,0:T(8,128)(2,1)S(1)} %gather_fusion.17), channel_id=1, source_target_pairs={{1,0},{2,1},{3,2},{4,3},{5,4},{6,5},{7,6},{8,7},{9,8},{10,9},{11,1... | collective-permute-start | bytes 884744 | tf_op jit(solution)/shard_map/ppermute | solution.py:18
  62.6 11.9 %collective-permute-start.7 = (bf16[2,2,64,576]{3,2,1,0:T(8,128)(2,1)S(1)}, bf16[2,2,64,576]{3,2,1,0:T(8,128)(2,1)S(1)}, u32[]{:S(2)}, u32[]{:S(2)}) collective-permute-start(bf16[2,2,64,576]{3,2,1,0:T(8,128)(2,1)S(1)} %gather_fusion.19), channel_id=1, source_target_pairs={{2,0},{3,1},{4,2},{5,3},{6,4},{7,5},{8,6},{9,7},{10,8},{11,9},{12,... | collective-permute-start | bytes 884744 | tf_op jit(solution)/shard_map/ppermute | solution.py:18
  67.8 7.8 %copy-start = (s32[16]{0:T(128)S(1)}, s32[16]{0:T(128)}, u32[]{:S(2)}) copy-start(s32[16]{0:T(128)} %param.18) | copy-start | bytes 196
  75.6 1.3 copy-start.9
  76.8 8.7 %copy-start.4 = (s32[1024]{0:T(1024)}, s32[1024]{0:T(1024)S(1)}, u32[]{:S(2)}) copy-start(s32[1024]{0:T(1024)S(1)} %pad_clamp_fusion.17) | copy-start | bytes 12292 | tf_op jit(solution)/shard_map/while
  99.2 0.7 copy-start.2
  100.0 0.7 copy-start.7
  100.0 1.4 copy-start.10
  101.4 1.3 copy-start.9
  102.7 8.7 %copy-start.4 = (s32[1024]{0:T(1024)}, s32[1024]{0:T(1024)S(1)}, u32[]{:S(2)}) copy-start(s32[1024]{0:T(1024)S(1)} %pad_clamp_fusion.17) | copy-start | bytes 12292 | tf_op jit(solution)/shard_map/while
  125.1 0.7 copy-start.2
  125.8 0.7 copy-start.7
  125.8 1.4 copy-start.10
  129.3 8.7 %copy-start.5 = (s32[1024]{0:T(1024)}, s32[1024]{0:T(1024)S(1)}, u32[]{:S(2)}) copy-start(s32[1024]{0:T(1024)S(1)} %pad_clamp_fusion.19) | copy-start | bytes 12292 | tf_op jit(solution)/shard_map/while
  151.7 0.7 copy-start.3
  152.4 0.6 copy-start.8
  155.6 8.7 %copy-start.5 = (s32[1024]{0:T(1024)}, s32[1024]{0:T(1024)S(1)}, u32[]{:S(2)}) copy-start(s32[1024]{0:T(1024)S(1)} %pad_clamp_fusion.19) | copy-start | bytes 12292 | tf_op jit(solution)/shard_map/while
  178.0 0.7 copy-start.3
  178.7 0.6 copy-start.8
  180.1 12.1 %copy-start.16 = (s32[16]{0:T(128)S(1)}, s32[16]{0:T(128)}, u32[]{:S(2)}) copy-start(s32[16]{0:T(128)} %copy-done.15) | copy-start | bytes 196
  180.8 17.8 %collective-permute-start.14 = (bf16[2,2,64,512]{3,2,1,0:T(8,128)(2,1)S(1)}, bf16[2,2,64,512]{3,2,1,0:T(8,128)(2,1)}, u32[]{:S(2)}, u32[]{:S(2)}) collective-permute-start(bf16[2,2,64,512]{3,2,1,0:T(8,128)(2,1)S(1)} %gather_fusion.24), channel_id=1, source_target_pairs={{2,0},{3,1},{4,2},{5,3},{6,4},{7,5},{8,6},{9,7},{10,8},{11,9},{12,... | collective-permute-start | bytes 786440 | tf_op jit(solution)/shard_map/ppermute | solution.py:18
  186.8 14.1 %collective-permute-start.15 = (bf16[2,2,64,512]{3,2,1,0:T(8,128)(2,1)S(1)}, bf16[2,2,64,512]{3,2,1,0:T(8,128)(2,1)}, u32[]{:S(2)}, u32[]{:S(2)}) collective-permute-start(bf16[2,2,64,512]{3,2,1,0:T(8,128)(2,1)S(1)} %gather_fusion.25), channel_id=1, source_target_pairs={{1,0},{2,1},{3,2},{4,3},{5,4},{6,5},{7,6},{8,7},{9,8},{10,9},{11,1... | collective-permute-start | bytes 786440 | tf_op jit(solution)/shard_map/ppermute | solution.py:18
  191.3 11.9 %collective-permute-start.16 = (bf16[2,2,64,512]{3,2,1,0:T(8,128)(2,1)S(1)}, bf16[2,2,64,512]{3,2,1,0:T(8,128)(2,1)}, u32[]{:S(2)}, u32[]{:S(2)}) collective-permute-start(bf16[2,2,64,512]{3,2,1,0:T(8,128)(2,1)S(1)} %gather_fusion.26), channel_id=1, source_target_pairs={{15,0},{0,1},{1,2},{2,3},{3,4},{4,5},{5,6},{6,7},{7,8},{8,9},{9,10... | collective-permute-start | bytes 786440 | tf_op jit(solution)/shard_map/ppermute | solution.py:18
  192.1 13.5 %collective-permute-start.17 = (bf16[2,2,64,512]{3,2,1,0:T(8,128)(2,1)S(1)}, bf16[2,2,64,512]{3,2,1,0:T(8,128)(2,1)S(1)}, u32[]{:S(2)}, u32[]{:S(2)}) collective-permute-start(bf16[2,2,64,512]{3,2,1,0:T(8,128)(2,1)S(1)} %gather_fusion.27), channel_id=1, source_target_pairs={{14,0},{15,1},{0,2},{1,3},{2,4},{3,5},{4,6},{5,7},{6,8},{7,9},{8,1... | collective-permute-start | bytes 786440 | tf_op jit(solution)/shard_map/ppermute | solution.py:18
  193.7 4.9 %copy-start.17 = (s32[2]{0:T(128)S(1)}, s32[2]{0:T(128)}, u32[]{:S(2)}) copy-start(s32[2]{0:T(128)} %get-tuple-element.397) | copy-start | bytes 28
  193.7 7.2 %copy-start.18 = (s32[2]{0:T(128)S(1)}, s32[2]{0:T(128)}, u32[]{:S(2)}) copy-start(s32[2]{0:T(128)} %get-tuple-element.395) | copy-start | bytes 28
  193.7 9.5 %copy-start.19 = (s32[2]{0:T(128)S(1)}, s32[2]{0:T(128)}, u32[]{:S(2)}) copy-start(s32[2]{0:T(128)} %get-tuple-element.393) | copy-start | bytes 28
  198.6 7.0 %copy-start.20 = (s32[2]{0:T(128)S(1)}, s32[2]{0:T(128)}, u32[]{:S(2)}) copy-start(s32[2]{0:T(128)} %get-tuple-element.391) | copy-start | bytes 28
where the time goes:
time: 210 us; the launch traced here: 208 us
  local copies, waits for them, and re-layouts  87.7 us (42%)
  matrix products  49 us (23%)
  starting transfers between devices  33.8 us (16%)
  waiting for transfers between devices  20.3 us (10%)
  other arithmetic  14.6 us (7%)
    ppermute x18, starting transfers between devices, passed_along(): return lax.ppermute(block, axis, route)  33.8 us
    ppermute x18, waiting for transfers between devices, passed_along(): return lax.ppermute(block, axis, route)  20.3 us
    dot_general x4, matrix products, attend_pack(): lax.dot_general(flat[:, :lat_width], prompt_latent, (((1,), (1,)), ((), (...  11.7 us
    dot_general x4, matrix products, attend_pack(): jnp.dot(shared_w.astype(jnp.bfloat16).reshape(pack * rows_per, prompt_len...  11.4 us
    gather x4, local copies, waits for them, and re-layouts, fetch_home(): all_query[spots]  11.1 us
    scatter x4, local copies, waits for them, and re-layouts, per_device(): final.at[jnp.where(claimed >= 0, claimed, members)]  9.18 us
    gather x4, local copies, waits for them, and re-layouts, fetch_home(): private_latent[cont_rows]  8.69 us
    gather x4, local copies, waits for them, and re-layouts, fetch_home(): all_keys[spots]  8.51 us
  transfers between devices with their start and end apart: 18, of which 6 were waited for; matrix products, arithmetic and copies ran while one was open for 44% of the time, Pallas kernels for 0%

commit v1 on v0

v1 whole, which is shorter than its diff:
```python
import functools
import math

import jax
import jax.numpy as jnp
from jax import lax
from jax.experimental import pallas as pl
from jax.experimental.pallas import tpu as pltpu
from jax.sharding import PartitionSpec as P

DR = 64
NOPE = 128
REACH = 2
TRANSFER_LIMIT = 2
FRESH_ROWS = 16
CHUNKS = 4
MESH = pl.DeviceIdType.MESH
OFFSETS = tuple(o for o in range(-REACH, REACH + 1) if o != 0)
NT = (((1,), (1,)), ((), ()))


def scores_of(q, latent, rope):
    width = latent.shape[1]
    s = lax.dot_general(q[:, :width], latent, NT, preferred_element_type=jnp.float32)
    return s + jnp.dot(q[:, width:], rope, preferred_element_type=jnp.float32)


def kernel(
    n, heads,
    slot_s, prompt_s, length_s, slot_v, q_hbm, nk_hbm, lat_hbm, rope_hbm, plat_hbm, prope_hbm,
    out_hbm,
    qin, qsend, qrecv, qg, nkg, lat, rope, prior_lat, prior_rope, plat, prope,
    m_ref, l_ref, acc_ref, res, osend, orecv, out_v,
    meta_v, meta_s, rank_s, order_s, qidx_s, src_s, osel_s,
    in_sem, meta_send, meta_recv, meta_local, q_send, q_recv, p_send, p_recv, o_send, o_recv, out_sem,
):
    me = lax.axis_index("seq")
    members, rows, width = qin.shape[0], res.shape[1], lat.shape[1]
    group = members // 2
    plen = lat.shape[0]
    chunk = plen // CHUNKS
    coef = (NOPE + DR) ** (-0.5) * math.log2(math.e)
    lo = me * members
    peers = [lax.rem(me + o + n, n) for o in OFFSETS]
    nxt = lax.rem(me + 1, n)
    last = len(OFFSETS) - 1

    local = [
        pltpu.make_async_copy(q_hbm, qin.at[:, pl.ds(0, rows), :], in_sem.at[0]),
        pltpu.make_async_copy(nk_hbm, qin.at[:, pl.ds(rows, FRESH_ROWS), :], in_sem.at[1]),
        pltpu.make_async_copy(plat_hbm, plat, in_sem.at[2]),
        pltpu.make_async_copy(prope_hbm, prope, in_sem.at[3]),
        pltpu.make_async_copy(lat_hbm, lat, in_sem.at[4]),
        pltpu.make_async_copy(rope_hbm, rope, in_sem.at[5]),
    ]
    for c in local:
        c.start()

    barrier = pltpu.get_barrier_semaphore()
    for peer in peers:
        pl.semaphore_signal(barrier, inc=1, device_id={"seq": peer}, device_id_type=MESH)
    pl.semaphore_wait(barrier, len(OFFSETS))

    meta = []
    for k in range(len(OFFSETS)):
        meta.append(pltpu.make_async_remote_copy(
            src_ref=slot_v, dst_ref=meta_v.at[k], send_sem=meta_send.at[k], recv_sem=meta_recv.at[k],
            device_id={"seq": peers[k]}, device_id_type=MESH))
        meta[k].start()

    prompt_copies = []
    for j in range(CHUNKS):
        part = pl.ds(j * chunk, chunk)
        prompt_copies.append((
            pltpu.make_async_remote_copy(
                src_ref=lat_hbm.at[part, :], dst_ref=prior_lat.at[part, :],
                send_sem=p_send.at[2 * j], recv_sem=p_recv.at[2 * j],
                device_id={"seq": nxt}, device_id_type=MESH),
            pltpu.make_async_remote_copy(
                src_ref=rope_hbm.at[:, part], dst_ref=prior_rope.at[:, part],
                send_sem=p_send.at[2 * j + 1], recv_sem=p_recv.at[2 * j + 1],
                device_id={"seq": nxt}, device_id_type=MESH),
        ))
    for c in prompt_copies[0]:
        c.start()

    zero = jnp.int32(0)

    def route(c, carry):
        own_count, prior_count, counts, sel = carry
        ns = slot_s[c]
        is_own = jnp.where(prompt_s[c] == me, 1, 0)
        rank = jnp.where(is_own == 1, own_count, group + prior_count)
        rank = jnp.minimum(rank, members - 1)
        rank_s[c] = rank
        place = jnp.where((ns >= lo) & (ns < lo + members), ns - lo, 0)
        counts, sel = list(counts), list(sel)
        for k in range(len(OFFSETS)):
            base = peers[k] * members
            hit = (ns >= base) & (ns < base + members)
            for r in range(TRANSFER_LIMIT):
                this = hit & (counts[k] == r)
                sel[k * TRANSFER_LIMIT + r] = jnp.where(this, rank, sel[k * TRANSFER_LIMIT + r])
                place = jnp.where(this, members + k * TRANSFER_LIMIT + r, place)
            counts[k] = counts[k] + jnp.where(hit, 1, 0)
        qidx_s[c] = place
        return own_count + is_own, prior_count + 1 - is_own, tuple(counts), tuple(sel)

    slots = len(OFFSETS) * TRANSFER_LIMIT
    routed = lax.fori_loop(
        0, members, route, (zero, zero, (zero,) * len(OFFSETS), (zero,) * slots))
    for i in range(slots):
        osel_s[i] = routed[3][i]

    def invert(p, _):
        order_s[p] = lax.fori_loop(
            0, members, lambda c, at: jnp.where(rank_s[c] == p, c, at), zero)
        return 0

    lax.fori_loop(0, members, invert, 0)

    for k in range(len(OFFSETS)):
        meta[k].wait_recv()
    to_smem = pltpu.make_async_copy(meta_v, meta_s, meta_local)
    to_smem.start()
    local[0].wait()
    local[1].wait()
    to_smem.wait()

    def claims(k):
        def step(c, carry):
            count, found = carry
            ns = meta_s[k, 0, c]
            hit = (ns >= lo) & (ns < lo + members)
            found = tuple(
                jnp.where(hit & (count == r), ns - lo, found[r]) for r in range(TRANSFER_LIMIT))
            return count + jnp.where(hit, 1, 0), found
        return lax.fori_loop(0, members, step, (zero, (zero - 1,) * TRANSFER_LIMIT))[1]

    claimed = []
    q_copies = []
    for k in range(len(OFFSETS)):
        found = claims(k)
        claimed.extend(found)
        for r in range(TRANSFER_LIMIT):
            qsend[k, r] = qin[jnp.maximum(found[r], 0)]
        span = pl.ds(k * TRANSFER_LIMIT, TRANSFER_LIMIT)
        q_copies.append(pltpu.make_async_remote_copy(
            src_ref=qsend.at[k], dst_ref=qrecv.at[span], send_sem=q_send.at[k], recv_sem=q_recv.at[k],
            device_id={"seq": peers[last - k]}, device_id_type=MESH))
        q_copies[k].start()
    for j in range(1, CHUNKS):
        for c in prompt_copies[j]:
            c.start()

    def sources(s, _):
        at = lax.fori_loop(
            0, members, lambda c, v: jnp.where(slot_s[c] == lo + s, rank_s[c], v), zero + members)
        for i in range(slots):
            at = jnp.where(claimed[i] == s, members + 1 + i, at)
        src_s[s] = at
        return 0

    lax.fori_loop(0, members, sources, 0)
    res[members] = jnp.zeros(res.shape[1:], res.dtype)

    for c in local[2:]:
        c.wait()
    for k in range(len(OFFSETS)):
        q_copies[k].wait_recv()

    lane = lax.broadcasted_iota(jnp.int32, (rows, plat.shape[1]), 1)
    fresh_col = lax.broadcasted_iota(jnp.int32, (rows, FRESH_ROWS), 1)
    fresh_row = lax.broadcasted_iota(jnp.int32, (rows, FRESH_ROWS), 0)
    fresh_ok = fresh_col * heads <= fresh_row
    first_lane = lane == 0

    def begin(p, _):
        c = order_s[p]
        at = qidx_s[c]
        moved = at >= members
        ext = jnp.where(moved, qrecv[jnp.maximum(at - members, 0)], qin[jnp.minimum(at, members - 1)])
        q = ext[:rows]
        nk = ext[rows:]
        span = pl.ds(pl.multiple_of(p * rows, rows), rows)
        qg[span, :] = q
        block = plat[c]
        s1 = jnp.where(lane < length_s[c], scores_of(q, block, prope[c]), -1e30)
        s2 = lax.dot_general(q, nk, NT, preferred_element_type=jnp.float32)
        s2 = jnp.where(fresh_ok, s2, -1e30)
        top = jnp.maximum(jnp.max(s1, axis=1, keepdims=True), jnp.max(s2, axis=1, keepdims=True))
        w1 = jnp.exp2((s1 - top) * coef)
        w2 = jnp.exp2((s2 - top) * coef)
        m_ref[span, :] = jnp.broadcast_to(top, (rows, m_ref.shape[1]))
        l_ref[span, :] = w1 + jnp.where(first_lane, jnp.sum(w2, axis=1, keepdims=True), 0.0)
        acc_ref[span, :] = jnp.dot(
            w1.astype(jnp.bfloat16), block, preferred_element_type=jnp.float32
        ) + jnp.dot(w2.astype(jnp.bfloat16), nk[:, :width], preferred_element_type=jnp.float32)
        return 0

    lax.fori_loop(0, members, begin, 0)

    rb = 2 * rows
    lanes = m_ref.shape[1]

    def shared(lat_ref, rope_ref, j, first):
        part = pl.ds(j * chunk, chunk)

        def step(b, _):
            span = pl.ds(pl.multiple_of(first + b * rb, rb), rb)
            s = scores_of(qg[span, :], lat_ref[part, :], rope_ref[:, part])
            before = m_ref[span, :]
            top = jnp.maximum(before, jnp.max(s, axis=1, keepdims=True))
            fade = jnp.exp2((before - top) * coef)
            pieces = [
                jnp.exp2((s[:, i * lanes:(i + 1) * lanes] - top) * coef)
                for i in range(chunk // lanes)
            ]
            m_ref[span, :] = top
            l_ref[span, :] = l_ref[span, :] * fade + functools.reduce(jnp.add, pieces)
            w = jnp.concatenate([x.astype(jnp.bfloat16) for x in pieces], axis=1)
            mix = jnp.dot(w, lat_ref[part, :], preferred_element_type=jnp.float32)
            acc_ref[span, :] = (
                acc_ref[span, :] * jnp.concatenate([fade] * (width // lanes), axis=1) + mix)
            return 0

        lax.fori_loop(0, group * rows // rb, step, 0)

    def finish(p, _):
        span = pl.ds(pl.multiple_of(p * rows, rows), rows)
        total = jnp.sum(l_ref[span, :], axis=1, keepdims=True)
        res[p] = (acc_ref[span, :] / total).astype(res.dtype)
        return 0

    for j in range(CHUNKS):
        shared(lat, rope, j, 0)
    lax.fori_loop(0, group, finish, 0)
    for j in range(CHUNKS):
        for c in prompt_copies[j]:
            c.wait_recv()
        shared(prior_lat, prior_rope, j, group * rows)
    lax.fori_loop(group, members, finish, 0)

    o_copies = []
    for k in range(len(OFFSETS)):
        for r in range(TRANSFER_LIMIT):
            osend[k, r] = res[osel_s[k * TRANSFER_LIMIT + r]]
        span = pl.ds(k * TRANSFER_LIMIT, TRANSFER_LIMIT)
        o_copies.append(pltpu.make_async_remote_copy(
            src_ref=osend.at[k], dst_ref=orecv.at[span], send_sem=o_send.at[k], recv_sem=o_recv.at[k],
            device_id={"seq": peers[k]}, device_id_type=MESH))
        o_copies[k].start()
    for k in range(len(OFFSETS)):
        o_copies[k].wait_recv()

    def place(s, _):
        at = src_s[s]
        out_v[s] = jnp.where(
            at > members, orecv[jnp.maximum(at - members - 1, 0)], res[jnp.minimum(at, members)])
        return 0

    half = members // 2
    writes = []
    for h in range(2):
        lax.fori_loop(h * half, (h + 1) * half, place, 0)
        writes.append(pltpu.make_async_copy(
            out_v.at[pl.ds(h * half, half)], out_hbm.at[pl.ds(h * half, half)], out_sem.at[h]))
        writes[h].start()
    for w in writes:
        w.wait()
    for c in meta + q_copies + o_copies:
        c.wait_send()
    for pair in prompt_copies:
        for c in pair:
            c.wait_send()


def per_device(
    prompt_latent, prompt_rope, private_latent, private_rope,
    lengths, survived, prompt_of, new_slot, queries, new_keys,
):
    n = lax.axis_size("seq")
    members, steps, heads, full = queries.shape
    rows = steps * heads
    width = prompt_latent.shape[2]
    plen = prompt_latent.shape[1]
    block = private_latent.shape[1]
    rot = full - width
    kinds = len(OFFSETS)
    slots = kinds * TRANSFER_LIMIT
    fresh = jnp.pad(new_keys, ((0, 0), (0, FRESH_ROWS - steps), (0, 0)))
    bf, f32, i32 = jnp.bfloat16, jnp.float32, jnp.int32
    ext = rows + FRESH_ROWS
    smem = pl.BlockSpec(memory_space=pltpu.SMEM)
    hbm = pl.BlockSpec(memory_space=pl.ANY)
    dma = pltpu.SemaphoreType.DMA
    out = pl.pallas_call(
        functools.partial(kernel, n, heads),
        out_shape=jax.ShapeDtypeStruct((members, rows, width), bf),
        in_specs=[smem, smem, smem, pl.BlockSpec(memory_space=pltpu.VMEM)] + [hbm] * 6,
        out_specs=hbm,
        scratch_shapes=[
            pltpu.VMEM((members, ext, full), bf),
            pltpu.VMEM((kinds, TRANSFER_LIMIT, ext, full), bf),
            pltpu.VMEM((slots, ext, full), bf),
            pltpu.VMEM((members * rows, full), bf),
            pltpu.VMEM((FRESH_ROWS, full), bf),
            pltpu.VMEM((plen, width), bf),
            pltpu.VMEM((rot, plen), bf),
            pltpu.VMEM((plen, width), bf),
            pltpu.VMEM((rot, plen), bf),
            pltpu.VMEM((members, block, width), bf),
            pltpu.VMEM((members, rot, block), bf),
            pltpu.VMEM((members * rows, block), f32),
            pltpu.VMEM((members * rows, block), f32),
            pltpu.VMEM((members * rows, width), f32),
            pltpu.VMEM((members + 1, rows, width), bf),
            pltpu.VMEM((kinds, TRANSFER_LIMIT, rows, width), bf),
            pltpu.VMEM((slots, rows, width), bf),
            pltpu.VMEM((members, rows, width), bf),
            pltpu.VMEM((kinds, 1, members), i32),
            pltpu.SMEM((kinds, 1, members), i32),
            pltpu.SMEM((members,), i32),
            pltpu.SMEM((members,), i32),
            pltpu.SMEM((members,), i32),
            pltpu.SMEM((members,), i32),
            pltpu.SMEM((slots,), i32),
            dma((6,)),
            dma((kinds,)),
            dma((kinds,)),
            dma(()),
            dma((kinds,)),
            dma((kinds,)),
            dma((2 * CHUNKS,)),
            dma((2 * CHUNKS,)),
            dma((kinds,)),
            dma((kinds,)),
            dma((2,)),
        ],
        compiler_params=pltpu.CompilerParams(
            collective_id=0, has_side_effects=True, vmem_limit_bytes=56 * 2**20),
    )(
        new_slot, prompt_of, lengths, new_slot.reshape(1, members),
        queries.reshape(members, rows, full), fresh,
        prompt_latent[0], prompt_rope[0], private_latent, private_rope,
    )
    return out.reshape(members, steps, heads, width)


def solution(mesh):
    lead = ("rep", "seq")
    return jax.shard_map(
        per_device,
        mesh=mesh,
        in_specs=(
            P(lead, None, None), P(lead, None, None), P(lead, None, None), P(lead, None, None),
            P(lead), P(lead), P(lead), P(lead),
            P(lead, None, None, None), P(lead, None, None),
        ),
        out_specs=P(lead, None, None, None),
        check_vma=False,
    )
```

time: 210 us -> 108 us (0.51)
  Pallas kernels: 0 us -> 102 us
  local copies, waits for them, and re-layouts: 87.7 us -> 4.67 us
  matrix products: 49 us -> 0 us
  starting transfers between devices: 33.8 us -> 0 us
  waiting for transfers between devices: 20.3 us -> 0 us
  other arithmetic: 14.6 us -> 0 us
    pallas_call x0 -> x1, Pallas kernels: none -> 102 us  [per_device(): pl.pallas_call(functools.partial(kernel, n, heads), out_shape=jax.ShapeDt...]
    gather x40 -> x0, local copies, waits for them, and re-layouts: 53.3 us -> none  [the longest x4 11.1 us: fetch_home(): all_query[spots]]
    dot_general x36 -> x0, matrix products: 49 us -> none  [the longest x4 11.7 us: attend_pack(): lax.dot_general(flat[:, :lat_width], prompt_latent, (((1,), (1,)), ((), (...]
    ppermute x18 -> x0, starting transfers between devices: 33.8 us -> none  [passed_along(): return lax.ppermute(block, axis, route)]
    ppermute x18 -> x0, waiting for transfers between devices: 20.3 us -> none  [passed_along(): return lax.ppermute(block, axis, route)]
    scatter x13 -> x0, local copies, waits for them, and re-layouts: 19.1 us -> none  [the longest x4 9.18 us: per_device(): final.at[jnp.where(claimed >= 0, claimed, members)]]
    unnamed x34 -> x1, local copies, waits for them, and re-layouts: 8.33 us -> 3.13 us
    reduce_sum x18 -> x0, other arithmetic: 4.61 us -> none  [the longest x4 3.02 us: attend_pack(): jnp.sum(shared_w, axis=2, keepdims=True)]
  transfers between devices with their start and end apart: 18 -> 0, of which waited for: 6 -> 0; matrix products, arithmetic and copies ran while one was open for 44% -> 0% of each run, Pallas kernels for 0% -> 0%
where the time goes in v1:
time: 108 us; the launch traced here: 107 us
  Pallas kernels  102 us (94%)
  local copies, waits for them, and re-layouts  4.67 us (4%)
    pallas_call x1, Pallas kernels, per_device(): pl.pallas_call(functools.partial(kernel, n, heads), out_shape=jax.ShapeDt...  102 us
    unnamed x1, local copies, waits for them, and re-layouts  3.13 us

profile of v1, /device:TPU:1, one launch (start us, length us, event | category | flops | bytes accessed | tf_op | source)
XLA Modules:
  0.0 106.5 jit_solution(14930848090623739460)
XLA Ops:
  0.0 1.5 %pad.4.nk_hbm = bf16[16,16,576]{2,1,0:T(8,128)(2,1)} pad(bf16[16,2,576]{2,1,0:T(2,128)(2,1)} %param.18, bf16[]{:T(256)} %constant.2.clone.1), padding=0_0x0_14x0_0 | pad | bytes 331778 | tf_op jit(solution)/shard_map/jit(_pad)/pad | solution.py:291
  1.5 101.8 %shard_map.91 = bf16[16,128,512]{2,1,0:T(8,128)(2,1)} custom-call(s32[16]{0:T(128)} %slot_s.1, s32[16]{0:T(128)} %prompt_s.1, s32[16]{0:T(128)} %length_s.1, s32[1,16]{1,0:T(1,128)} %bitcast.9, bf16[16,128,576]{2,1,0:T(8,128)(2,1)} %bitcast.6, bf16[16,16,576]{2,1,0:T(8,128)(2,1)} %pad.4.nk_hbm, bf16[2048,512]{1,0:T(8,128)(2,1)} %bitcast.7, ...), custom_call_target="tpu_custom_call" | custom-call | tf_op jit(solution)/shard_map/pallas_call | solution.py:297
  103.4 3.1 %copy.11 = bf16[16,2,64,512]{3,2,1,0:T(8,128)(2,1)} copy(bf16[16,2,64,512]{3,2,1,0:T(8,128)(2,1)} %bitcast.5) | data formatting | bytes 4194304

commit v2 on v1

--- a/solution.py
+++ b/solution.py
@@ -19,23 +19,25 @@
 NT = (((1,), (1,)), ((), ()))
 
 
-def scores_of(q, latent, rope):
-    width = latent.shape[1]
-    s = lax.dot_general(q[:, :width], latent, NT, preferred_element_type=jnp.float32)
-    return s + jnp.dot(q[:, width:], rope, preferred_element_type=jnp.float32)
+def scores_of(q_lat, q_rot, latent, rope):
+    s = lax.dot_general(q_lat, latent, NT, preferred_element_type=jnp.float32)
+    return s + jnp.dot(q_rot, rope, preferred_element_type=jnp.float32)
 
 
 def kernel(
     n, heads,
     slot_s, prompt_s, length_s, slot_v, q_hbm, nk_hbm, lat_hbm, rope_hbm, plat_hbm, prope_hbm,
-    out_hbm,
-    qin, qsend, qrecv, qg, nkg, lat, rope, prior_lat, prior_rope, plat, prope,
-    m_ref, l_ref, acc_ref, res, osend, orecv, out_v,
-    meta_v, meta_s, rank_s, order_s, qidx_s, src_s, osel_s,
+    all_hbm, src_s,
+    qin, nkin, lsend, rsend, ksend, lrecv, rrecv, krecv, qg_lat, qg_rot,
+    lat, rope, prior_lat, prior_rope, plat, prope,
+    m_ref, l_ref, acc_ref, res, osend,
+    meta_v, meta_s, rank_s, order_s, qidx_s, osel_s,
     in_sem, meta_send, meta_recv, meta_local, q_send, q_recv, p_send, p_recv, o_send, o_recv, out_sem,
 ):
     me = lax.axis_index("seq")
     members, rows, width = qin.shape[0], res.shape[1], lat.shape[1]
+    rot = rope.shape[0]
+    steps = rows // heads
     group = members // 2
     plen = lat.shape[0]
     chunk = plen // CHUNKS
@@ -46,8 +48,8 @@
     last = len(OFFSETS) - 1
 
     local = [
-        pltpu.make_async_copy(q_hbm, qin.at[:, pl.ds(0, rows), :], in_sem.at[0]),
-        pltpu.make_async_copy(nk_hbm, qin.at[:, pl.ds(rows, FRESH_ROWS), :], in_sem.at[1]),
+        pltpu.make_async_copy(q_hbm, qin, in_sem.at[0]),
+        pltpu.make_async_copy(nk_hbm, nkin, in_sem.at[1]),
         pltpu.make_async_copy(plat_hbm, plat, in_sem.at[2]),
         pltpu.make_async_copy(prope_hbm, prope, in_sem.at[3]),
         pltpu.make_async_copy(lat_hbm, lat, in_sem.at[4]),
@@ -142,13 +144,21 @@
     for k in range(len(OFFSETS)):
         found = claims(k)
         claimed.extend(found)
+        spots = [jnp.maximum(f, 0) for f in found]
         for r in range(TRANSFER_LIMIT):
-            qsend[k, r] = qin[jnp.maximum(found[r], 0)]
-        span = pl.ds(k * TRANSFER_LIMIT, TRANSFER_LIMIT)
-        q_copies.append(pltpu.make_async_remote_copy(
-            src_ref=qsend.at[k], dst_ref=qrecv.at[span], send_sem=q_send.at[k], recv_sem=q_recv.at[k],
-            device_id={"seq": peers[last - k]}, device_id_type=MESH))
-        q_copies[k].start()
+            lsend[k, r] = qin[spots[r]][:, :width]
+        rsend[k] = jnp.concatenate([qin[at][:, width:] for at in spots], axis=1)
+        ksend[k] = functools.reduce(jnp.add, [nkin[at, r] for r, at in enumerate(spots)])
+        group_copies = [
+            pltpu.make_async_remote_copy(
+                src_ref=src.at[k], dst_ref=dst.at[k], send_sem=q_send.at[3 * k + i],
+                recv_sem=q_recv.at[3 * k + i],
+                device_id={"seq": peers[last - k]}, device_id_type=MESH)
+            for i, (src, dst) in enumerate(((lsend, lrecv), (rsend, rrecv), (ksend, krecv)))
+        ]
+        for c in group_copies:
+            c.start()
+        q_copies.extend(group_copies)
     for j in range(1, CHUNKS):
         for c in prompt_copies[j]:
             c.start()
@@ -166,113 +176,132 @@
 
     for c in local[2:]:
         c.wait()
-    for k in range(len(OFFSETS)):
-        q_copies[k].wait_recv()
+    for c in q_copies:
+        c.wait_recv()
 
     lane = lax.broadcasted_iota(jnp.int32, (rows, plat.shape[1]), 1)
     fresh_col = lax.broadcasted_iota(jnp.int32, (rows, FRESH_ROWS), 1)
     fresh_row = lax.broadcasted_iota(jnp.int32, (rows, FRESH_ROWS), 0)
-    fresh_ok = fresh_col * heads <= fresh_row
     first_lane = lane == 0
-
-    def begin(p, _):
+    share = FRESH_ROWS // TRANSFER_LIMIT
+
+    def begin_one(p):
         c = order_s[p]
         at = qidx_s[c]
         moved = at >= members
-        ext = jnp.where(moved, qrecv[jnp.maximum(at - members, 0)], qin[jnp.minimum(at, members - 1)])
-        q = ext[:rows]
-        nk = ext[rows:]
-        span = pl.ds(pl.multiple_of(p * rows, rows), rows)
-        qg[span, :] = q
+        far = jnp.maximum(at - members, 0)
+        lane_k, turn = far // TRANSFER_LIMIT, far % TRANSFER_LIMIT
+        near = jnp.minimum(at, members - 1)
+        home = qin[near]
+        q_lat = jnp.where(moved, lrecv[lane_k, turn], home[:, :width])
+        packed = rrecv[lane_k]
+        far_rot = packed[:, :rot]
+        for r in range(1, TRANSFER_LIMIT):
+            far_rot = jnp.where(turn == r, packed[:, r * rot:(r + 1) * rot], far_rot)
+        q_rot = jnp.where(moved, far_rot, home[:, width:])
+        nk = jnp.where(moved, krecv[lane_k], nkin[near, 0])
+        base = jnp.where(moved, turn * share, 0)
         block = plat[c]
-        s1 = jnp.where(lane < length_s[c], scores_of(q, block, prope[c]), -1e30)
-        s2 = lax.dot_general(q, nk, NT, preferred_element_type=jnp.float32)
-        s2 = jnp.where(fresh_ok, s2, -1e30)
+        s1 = jnp.where(lane < length_s[c], scores_of(q_lat, q_rot, block, prope[c]), -1e30)
+        s2 = lax.dot_general(q_lat, nk[:, :width], NT, preferred_element_type=jnp.float32)
+        s2 = s2 + lax.dot_general(q_rot, nk[:, width:], NT, preferred_element_type=jnp.float32)
+        new = fresh_col - base
+        s2 = jnp.where((new >= 0) & (new < steps) & (new * heads <= fresh_row), s2, -1e30)
         top = jnp.maximum(jnp.max(s1, axis=1, keepdims=True), jnp.max(s2, axis=1, keepdims=True))
         w1 = jnp.exp2((s1 - top) * coef)
         w2 = jnp.exp2((s2 - top) * coef)
-        m_ref[span, :] = jnp.broadcast_to(top, (rows, m_ref.shape[1]))
-        l_ref[span, :] = w1 + jnp.where(first_lane, jnp.sum(w2, axis=1, keepdims=True), 0.0)
-        acc_ref[span, :] = jnp.dot(
+        total = w1 + jnp.where(first_lane, jnp.sum(w2, axis=1, keepdims=True), 0.0)
+        mix = jnp.dot(
             w1.astype(jnp.bfloat16), block, preferred_element_type=jnp.float32
         ) + jnp.dot(w2.astype(jnp.bfloat16), nk[:, :width], preferred_element_type=jnp.float32)
+        return q_lat, q_rot, jnp.broadcast_to(top, (rows, m_ref.shape[1])), total, mix
+
+    def begin(b, _):
+        made = [begin_one(2 * b + u) for u in range(2)]
+        for u in range(2):
+            span = pl.ds(pl.multiple_of((2 * b + u) * rows, rows), rows)
+            for ref, value in zip((qg_lat, qg_rot, m_ref, l_ref, acc_ref), made[u]):
+                ref[span, :] = value
         return 0
 
-    lax.fori_loop(0, members, begin, 0)
+    lax.fori_loop(0, members // 2, begin, 0)
 
     rb = 2 * rows
     lanes = m_ref.shape[1]
 
-    def shared(lat_ref, rope_ref, j, first):
-        part = pl.ds(j * chunk, chunk)
+    def shared(lat_ref, rope_ref, js, first, final):
+        parts = [pl.ds(j * chunk, chunk) for j in js]
 
         def step(b, _):
-            span = pl.ds(pl.multiple_of(first + b * rb, rb), rb)
-            s = scores_of(qg[span, :], lat_ref[part, :], rope_ref[:, part])
-            before = m_ref[span, :]
-            top = jnp.maximum(before, jnp.max(s, axis=1, keepdims=True))
+            span = pl.ds(pl.multiple_of((first + 2 * b) * rows, rb), rb)
+            q_lat, q_rot, before = qg_lat[span, :], qg_rot[span, :], m_ref[span, :]
+            tiles = []
+            for part in parts:
+                s = scores_of(q_lat, q_rot, lat_ref[part, :], rope_ref[:, part])
+                tiles.append([s[:, i * lanes:(i + 1) * lanes] for i in range(chunk // lanes)])
+            peak = functools.reduce(jnp.maximum, [t for group_ in tiles for t in group_])
+            top = jnp.maximum(before, jnp.max(peak, axis=1, keepdims=True))
             fade = jnp.exp2((before - top) * coef)
-            pieces = [
-                jnp.exp2((s[:, i * lanes:(i + 1) * lanes] - top) * coef)
-                for i in range(chunk // lanes)
-            ]
-            m_ref[span, :] = top
-            l_ref[span, :] = l_ref[span, :] * fade + functools.reduce(jnp.add, pieces)
-            w = jnp.concatenate([x.astype(jnp.bfloat16) for x in pieces], axis=1)
-            mix = jnp.dot(w, lat_ref[part, :], preferred_element_type=jnp.float32)
-            acc_ref[span, :] = (
-                acc_ref[span, :] * jnp.concatenate([fade] * (width // lanes), axis=1) + mix)
+            total = l_ref[span, :] * fade
+            mix = acc_ref[span, :] * jnp.concatenate([fade] * (width // lanes), axis=1)
+            for part, group_ in zip(parts, tiles):
+                pieces = [jnp.exp2((t - top) * coef) for t in group_]
+                total = total + functools.reduce(jnp.add, pieces)
+                w = jnp.concatenate([x.astype(jnp.bfloat16) for x in pieces], axis=1)
+                mix = mix + jnp.dot(w, lat_ref[part, :], preferred_element_type=jnp.float32)
+            if final:
+                out = (mix * (1.0 / jnp.sum(total, axis=1, keepdims=True))).astype(res.dtype)
+                for u in range(2):
+                    res[first + 2 * b + u] = out[u * rows:(u + 1) * rows]
+            else:
+                m_ref[span, :] = top
+                l_ref[span, :] = total
+                acc_ref[span, :] = mix
             return 0
 
-        lax.fori_loop(0, group * rows // rb, step, 0)
-
-    def finish(p, _):
-        span = pl.ds(pl.multiple_of(p * rows, rows), rows)
-        total = jnp.sum(l_ref[span, :], axis=1, keepdims=True)
-        res[p] = (acc_ref[span, :] / total).astype(res.dtype)
-        return 0
-
-    for j in range(CHUNKS):
-        shared(lat, rope, j, 0)
-    lax.fori_loop(0, group, finish, 0)
-    for j in range(CHUNKS):
-        for c in prompt_copies[j]:
-            c.wait_recv()
-        shared(prior_lat, prior_rope, j, group * rows)
-    lax.fori_loop(group, members, finish, 0)
+        lax.fori_loop(0, group // 2, step, 0)
+
+    def arrive(js):
+        for j in js:
+            for c in prompt_copies[j]:
+                c.wait_recv()
+
+    shared(lat, rope, range(CHUNKS), 0, True)
+    arrive(range(CHUNKS - 1))
+    shared(prior_lat, prior_rope, range(CHUNKS - 1), group, False)
+    arrive((CHUNKS - 1,))
+    shared(prior_lat, prior_rope, (CHUNKS - 1,), group, True)
 
     o_copies = []
     for k in range(len(OFFSETS)):
         for r in range(TRANSFER_LIMIT):
             osend[k, r] = res[osel_s[k * TRANSFER_LIMIT + r]]
-        span = pl.ds(k * TRANSFER_LIMIT, TRANSFER_LIMIT)
+        span = pl.ds(members + 1 + k * TRANSFER_LIMIT, TRANSFER_LIMIT)
         o_copies.append(pltpu.make_async_remote_copy(
-            src_ref=osend.at[k], dst_ref=orecv.at[span], send_sem=o_send.at[k], recv_sem=o_recv.at[k],
+            src_ref=osend.at[k], dst_ref=all_hbm.at[span], send_sem=o_send.at[k], recv_sem=o_recv.at[k],
             device_id={"seq": peers[k]}, device_id_type=MESH))
         o_copies[k].start()
-    for k in range(len(OFFSETS)):
-        o_copies[k].wait_recv()
-
-    def place(s, _):
-        at = src_s[s]
-        out_v[s] = jnp.where(
-            at > members, orecv[jnp.maximum(at - members - 1, 0)], res[jnp.minimum(at, members)])
-        return 0
-
-    half = members // 2
-    writes = []
-    for h in range(2):
-        lax.fori_loop(h * half, (h + 1) * half, place, 0)
-        writes.append(pltpu.make_async_copy(
-            out_v.at[pl.ds(h * half, half)], out_hbm.at[pl.ds(h * half, half)], out_sem.at[h]))
-        writes[h].start()
-    for w in writes:
-        w.wait()
-    for c in meta + q_copies + o_copies:
+    keep = pltpu.make_async_copy(res, all_hbm.at[pl.ds(0, members + 1)], out_sem)
+    keep.start()
+    for c in meta + q_copies:
         c.wait_send()
     for pair in prompt_copies:
         for c in pair:
             c.wait_send()
+    keep.wait()
+    for c in o_copies:
+        c.wait()
+
+
+def place_kernel(src_s, all_hbm, out_hbm, sem):
+    copies = [
+        pltpu.make_async_copy(all_hbm.at[src_s[s]], out_hbm.at[s], sem.at[s])
+        for s in range(out_hbm.shape[0])
+    ]
+    for c in copies:
+        c.start()
+    for c in copies:
+        c.wait()
 
 
 def per_device(
@@ -288,23 +317,33 @@
     rot = full - width
     kinds = len(OFFSETS)
     slots = kinds * TRANSFER_LIMIT
-    fresh = jnp.pad(new_keys, ((0, 0), (0, FRESH_ROWS - steps), (0, 0)))
+    share = FRESH_ROWS // TRANSFER_LIMIT
+    fresh = jnp.stack([
+        jnp.pad(new_keys, ((0, 0), (r * share, FRESH_ROWS - steps - r * share), (0, 0)))
+        for r in range(TRANSFER_LIMIT)
+    ], axis=1)
     bf, f32, i32 = jnp.bfloat16, jnp.float32, jnp.int32
-    ext = rows + FRESH_ROWS
     smem = pl.BlockSpec(memory_space=pltpu.SMEM)
     hbm = pl.BlockSpec(memory_space=pl.ANY)
     dma = pltpu.SemaphoreType.DMA
-    out = pl.pallas_call(
+    everything, src = pl.pallas_call(
         functools.partial(kernel, n, heads),
-        out_shape=jax.ShapeDtypeStruct((members, rows, width), bf),
+        out_shape=(
+            jax.ShapeDtypeStruct((members + 1 + slots, rows, width), bf),
+            jax.ShapeDtypeStruct((members,), i32)),
         in_specs=[smem, smem, smem, pl.BlockSpec(memory_space=pltpu.VMEM)] + [hbm] * 6,
-        out_specs=hbm,
+        out_specs=(hbm, smem),
         scratch_shapes=[
-            pltpu.VMEM((members, ext, full), bf),
-            pltpu.VMEM((kinds, TRANSFER_LIMIT, ext, full), bf),
-            pltpu.VMEM((slots, ext, full), bf),
-            pltpu.VMEM((members * rows, full), bf),
-            pltpu.VMEM((FRESH_ROWS, full), bf),
+            pltpu.VMEM((members, rows, full), bf),
+            pltpu.VMEM((members, TRANSFER_LIMIT, FRESH_ROWS, full), bf),
+            pltpu.VMEM((kinds, TRANSFER_LIMIT, rows, width), bf),
+            pltpu.VMEM((kinds, rows, TRANSFER_LIMIT * rot), bf),
+            pltpu.VMEM((kinds, FRESH_ROWS, full), bf),
+            pltpu.VMEM((kinds, TRANSFER_LIMIT, rows, width), bf),
+            pltpu.VMEM((kinds, rows, TRANSFER_LIMIT * rot), bf),
+            pltpu.VMEM((kinds, FRESH_ROWS, full), bf),
+            pltpu.VMEM((members * rows, width), bf),
+            pltpu.VMEM((members * rows, rot), bf),
             pltpu.VMEM((plen, width), bf),
             pltpu.VMEM((rot, plen), bf),
             pltpu.VMEM((plen, width), bf),
@@ -316,11 +355,8 @@
             pltpu.VMEM((members * rows, width), f32),
             pltpu.VMEM((members + 1, rows, width), bf),
             pltpu.VMEM((kinds, TRANSFER_LIMIT, rows, width), bf),
-            pltpu.VMEM((slots, rows, width), bf),
-            pltpu.VMEM((members, rows, width), bf),
             pltpu.VMEM((kinds, 1, members), i32),
             pltpu.SMEM((kinds, 1, members), i32),
-            pltpu.SMEM((members,), i32),
             pltpu.SMEM((members,), i32),
             pltpu.SMEM((members,), i32),
             pltpu.SMEM((members,), i32),
@@ -329,13 +365,13 @@
             dma((kinds,)),
             dma((kinds,)),
             dma(()),
-            dma((kinds,)),
-            dma((kinds,)),
+            dma((3 * kinds,)),
+            dma((3 * kinds,)),
             dma((2 * CHUNKS,)),
             dma((2 * CHUNKS,)),
             dma((kinds,)),
             dma((kinds,)),
-            dma((2,)),
+            dma(()),
         ],
         compiler_params=pltpu.CompilerParams(
             collective_id=0, has_side_effects=True, vmem_limit_bytes=56 * 2**20),
@@ -344,6 +380,13 @@
         queries.reshape(members, rows, full), fresh,
         prompt_latent[0], prompt_rope[0], private_latent, private_rope,
     )
+    out = pl.pallas_call(
+        place_kernel,
+        out_shape=jax.ShapeDtypeStruct((members, rows, width), bf),
+        in_specs=[smem, hbm],
+        out_specs=hbm,
+        scratch_shapes=[dma((members,))],
+    )(src, everything)
     return out.reshape(members, steps, heads, width)
 
 

time: 108 us -> 159 us (1.47)
  Pallas kernels: 102 us -> 157 us
  local copies, waits for them, and re-layouts: 4.67 us -> 0.93 us
    pallas_call x1 -> x2, Pallas kernels: 102 us -> 157 us  [the longest x1 91.4 us: per_device(): pl.pallas_call(functools.partial(kernel, n, heads), out_shape=(jax.ShapeD...]
    unnamed x1 -> x0, local copies, waits for them, and re-layouts: 3.13 us -> none
where the time goes in v2:
time: 159 us
  Pallas kernels  157 us (99%)
    pallas_call x1, Pallas kernels, per_device(): pl.pallas_call(functools.partial(kernel, n, heads), out_shape=(jax.ShapeD...  91.4 us
    pallas_call x1, Pallas kernels, per_device(): pl.pallas_call(place_kernel, out_shape=jax.ShapeDtypeStruct((members, row...  65.4 us

profile of v2, /device:TPU:1, one launch (start us, length us, event | category | flops | bytes accessed | tf_op | source)
XLA Modules:
  0.0 158.7 jit_solution(14121525099185245038)
XLA Ops:
  0.0 0.9 pad_bitcast_fusion.1
  0.9 0.9 pad_maximum_fusion.nk_hbm
  1.9 91.4 %shard_map.91 = (bf16[25,128,512]{2,1,0:T(8,128)(2,1)}, s32[16]{0:T(128)}) custom-call(s32[16]{0:T(128)} %slot_s.1, s32[16]{0:T(128)} %prompt_s.1, s32[16]{0:T(128)} %length_s.1, s32[1,16]{1,0:T(1,128)} %bitcast.12, bf16[16,128,576]{2,1,0:T(8,128)(2,1)} %bitcast.9, bf16[16,2,16,576]{3,2,1,0:T(8,128)(2,1)} %pad_maximum_fusion.nk_hbm, ...), custom_call_target="tpu_custom_call" | custom-call | tf_op jit(solution)/shard_map/pallas_call | solution.py:329
  93.3 65.4 %shard_map.92 = bf16[16,128,512]{2,1,0:T(8,128)(2,1)} custom-call(s32[16]{0:T(128)} %get-tuple-element.7.src_s, bf16[25,128,512]{2,1,0:T(8,128)(2,1)} %get-tuple-element.8.all_hbm), custom_call_target="tpu_custom_call" | custom-call | tf_op jit(solution)/shard_map/pallas_call | solution.py:383

commit v3 on v2

--- a/solution.py
+++ b/solution.py
@@ -87,40 +87,6 @@
         c.start()
 
     zero = jnp.int32(0)
-
-    def route(c, carry):
-        own_count, prior_count, counts, sel = carry
-        ns = slot_s[c]
-        is_own = jnp.where(prompt_s[c] == me, 1, 0)
-        rank = jnp.where(is_own == 1, own_count, group + prior_count)
-        rank = jnp.minimum(rank, members - 1)
-        rank_s[c] = rank
-        place = jnp.where((ns >= lo) & (ns < lo + members), ns - lo, 0)
-        counts, sel = list(counts), list(sel)
-        for k in range(len(OFFSETS)):
-            base = peers[k] * members
-            hit = (ns >= base) & (ns < base + members)
-            for r in range(TRANSFER_LIMIT):
-                this = hit & (counts[k] == r)
-                sel[k * TRANSFER_LIMIT + r] = jnp.where(this, rank, sel[k * TRANSFER_LIMIT + r])
-                place = jnp.where(this, members + k * TRANSFER_LIMIT + r, place)
-            counts[k] = counts[k] + jnp.where(hit, 1, 0)
-        qidx_s[c] = place
-        return own_count + is_own, prior_count + 1 - is_own, tuple(counts), tuple(sel)
-
-    slots = len(OFFSETS) * TRANSFER_LIMIT
-    routed = lax.fori_loop(
-        0, members, route, (zero, zero, (zero,) * len(OFFSETS), (zero,) * slots))
-    for i in range(slots):
-        osel_s[i] = routed[3][i]
-
-    def invert(p, _):
-        order_s[p] = lax.fori_loop(
-            0, members, lambda c, at: jnp.where(rank_s[c] == p, c, at), zero)
-        return 0
-
-    lax.fori_loop(0, members, invert, 0)
-
     for k in range(len(OFFSETS)):
         meta[k].wait_recv()
     to_smem = pltpu.make_async_copy(meta_v, meta_s, meta_local)
@@ -159,9 +125,39 @@
         for c in group_copies:
             c.start()
         q_copies.extend(group_copies)
-    for j in range(1, CHUNKS):
-        for c in prompt_copies[j]:
-            c.start()
+
+    def route(c, carry):
+        own_count, prior_count, counts, sel = carry
+        ns = slot_s[c]
+        is_own = jnp.where(prompt_s[c] == me, 1, 0)
+        rank = jnp.where(is_own == 1, own_count, group + prior_count)
+        rank = jnp.minimum(rank, members - 1)
+        rank_s[c] = rank
+        place = jnp.where((ns >= lo) & (ns < lo + members), ns - lo, 0)
+        counts, sel = list(counts), list(sel)
+        for k in range(len(OFFSETS)):
+            base = peers[k] * members
+            hit = (ns >= base) & (ns < base + members)
+            for r in range(TRANSFER_LIMIT):
+                this = hit & (counts[k] == r)
+                sel[k * TRANSFER_LIMIT + r] = jnp.where(this, rank, sel[k * TRANSFER_LIMIT + r])
+                place = jnp.where(this, members + k * TRANSFER_LIMIT + r, place)
+            counts[k] = counts[k] + jnp.where(hit, 1, 0)
+        qidx_s[c] = place
+        return own_count + is_own, prior_count + 1 - is_own, tuple(counts), tuple(sel)
+
+    slots = len(OFFSETS) * TRANSFER_LIMIT
+    routed = lax.fori_loop(
+        0, members, route, (zero, zero, (zero,) * len(OFFSETS), (zero,) * slots))
+    for i in range(slots):
+        osel_s[i] = routed[3][i]
+
+    def invert(p, _):
+        order_s[p] = lax.fori_loop(
+            0, members, lambda c, at: jnp.where(rank_s[c] == p, c, at), zero)
+        return 0
+
+    lax.fori_loop(0, members, invert, 0)
 
     def sources(s, _):
         at = lax.fori_loop(
@@ -174,6 +170,11 @@
     lax.fori_loop(0, members, sources, 0)
     res[members] = jnp.zeros(res.shape[1:], res.dtype)
 
+    for c in q_copies:
+        c.wait_send()
+    for j in range(1, CHUNKS):
+        for c in prompt_copies[j]:
+            c.start()
     for c in local[2:]:
         c.wait()
     for c in q_copies:
@@ -283,7 +284,7 @@
         o_copies[k].start()
     keep = pltpu.make_async_copy(res, all_hbm.at[pl.ds(0, members + 1)], out_sem)
     keep.start()
-    for c in meta + q_copies:
+    for c in meta:
         c.wait_send()
     for pair in prompt_copies:
         for c in pair:
@@ -293,14 +294,20 @@
         c.wait()
 
 
-def place_kernel(src_s, all_hbm, out_hbm, sem):
-    copies = [
-        pltpu.make_async_copy(all_hbm.at[src_s[s]], out_hbm.at[s], sem.at[s])
-        for s in range(out_hbm.shape[0])
+def place_kernel(src_s, all_hbm, out_hbm, block, in_sem, out_sem):
+    members = out_hbm.shape[0]
+    reads = [
+        pltpu.make_async_copy(all_hbm.at[src_s[s]], block.at[s], in_sem.at[s]) for s in range(members)
     ]
-    for c in copies:
+    writes = [
+        pltpu.make_async_copy(block.at[s], out_hbm.at[s], out_sem.at[s]) for s in range(members)
+    ]
+    for c in reads:
         c.start()
-    for c in copies:
+    for read, write in zip(reads, writes):
+        read.wait()
+        write.start()
+    for c in writes:
         c.wait()
 
 
@@ -385,7 +392,7 @@
         out_shape=jax.ShapeDtypeStruct((members, rows, width), bf),
         in_specs=[smem, hbm],
         out_specs=hbm,
-        scratch_shapes=[dma((members,))],
+        scratch_shapes=[pltpu.VMEM((members, rows, width), bf), dma((members,)), dma((members,))],
     )(src, everything)
     return out.reshape(members, steps, heads, width)
 

time: 159 us -> 93.4 us (0.59)
  Pallas kernels: 157 us -> 91.3 us
    pallas_call x1, Pallas kernels: 65.4 us -> 3.24 us  [per_device(): pl.pallas_call(place_kernel, out_shape=jax.ShapeDtypeStruct((members, row...]
    pallas_call x1, Pallas kernels: 91.4 us -> 88 us  [per_device(): pl.pallas_call(functools.partial(kernel, n, heads), out_shape=(jax.ShapeD...]
where the time goes in v3:
time: 93.4 us; the launch traced here: 93.1 us
  Pallas kernels  91.3 us (98%)
    pallas_call x1, Pallas kernels, per_device(): pl.pallas_call(functools.partial(kernel, n, heads), out_shape=(jax.ShapeD...  88 us
    pallas_call x1, Pallas kernels, per_device(): pl.pallas_call(place_kernel, out_shape=jax.ShapeDtypeStruct((members, row...  3.24 us

profile of v3, /device:TPU:1, one launch (start us, length us, event | category | flops | bytes accessed | tf_op | source)
XLA Modules:
  0.0 93.1 jit_solution(796989193986107457)
XLA Ops:
  0.0 0.9 pad_bitcast_fusion.1
  0.9 0.9 pad_maximum_fusion.nk_hbm
  1.9 88.0 %shard_map.91 = (bf16[25,128,512]{2,1,0:T(8,128)(2,1)}, s32[16]{0:T(128)}) custom-call(s32[16]{0:T(128)} %slot_s.1, s32[16]{0:T(128)} %prompt_s.1, s32[16]{0:T(128)} %length_s.1, s32[1,16]{1,0:T(1,128)} %bitcast.12, bf16[16,128,576]{2,1,0:T(8,128)(2,1)} %bitcast.9, bf16[16,2,16,576]{3,2,1,0:T(8,128)(2,1)} %pad_maximum_fusion.nk_hbm, ...), custom_call_target="tpu_custom_call" | custom-call | tf_op jit(solution)/shard_map/pallas_call | solution.py:336
  89.9 3.2 %shard_map.92 = bf16[16,128,512]{2,1,0:T(8,128)(2,1)} custom-call(s32[16]{0:T(128)} %get-tuple-element.7.src_s, bf16[25,128,512]{2,1,0:T(8,128)(2,1)} %get-tuple-element.8.all_hbm), custom_call_target="tpu_custom_call" | custom-call | tf_op jit(solution)/shard_map/pallas_call | solution.py:390

commit v4 on v3

--- a/solution.py
+++ b/solution.py
@@ -218,14 +218,14 @@
         return q_lat, q_rot, jnp.broadcast_to(top, (rows, m_ref.shape[1])), total, mix
 
     def begin(b, _):
-        made = [begin_one(2 * b + u) for u in range(2)]
-        for u in range(2):
-            span = pl.ds(pl.multiple_of((2 * b + u) * rows, rows), rows)
+        made = [begin_one(4 * b + u) for u in range(4)]
+        for u in range(4):
+            span = pl.ds(pl.multiple_of((4 * b + u) * rows, rows), rows)
             for ref, value in zip((qg_lat, qg_rot, m_ref, l_ref, acc_ref), made[u]):
                 ref[span, :] = value
         return 0
 
-    lax.fori_loop(0, members // 2, begin, 0)
+    lax.fori_loop(0, members // 4, begin, 0)
 
     rb = 2 * rows
     lanes = m_ref.shape[1]
@@ -233,7 +233,7 @@
     def shared(lat_ref, rope_ref, js, first, final):
         parts = [pl.ds(j * chunk, chunk) for j in js]
 
-        def step(b, _):
+        def mixed(b):
             span = pl.ds(pl.multiple_of((first + 2 * b) * rows, rb), rb)
             q_lat, q_rot, before = qg_lat[span, :], qg_rot[span, :], m_ref[span, :]
             tiles = []
@@ -250,17 +250,23 @@
                 total = total + functools.reduce(jnp.add, pieces)
                 w = jnp.concatenate([x.astype(jnp.bfloat16) for x in pieces], axis=1)
                 mix = mix + jnp.dot(w, lat_ref[part, :], preferred_element_type=jnp.float32)
-            if final:
-                out = (mix * (1.0 / jnp.sum(total, axis=1, keepdims=True))).astype(res.dtype)
-                for u in range(2):
-                    res[first + 2 * b + u] = out[u * rows:(u + 1) * rows]
-            else:
-                m_ref[span, :] = top
-                l_ref[span, :] = total
-                acc_ref[span, :] = mix
+            return span, top, total, mix
+
+        def step(pair, _):
+            made = [mixed(2 * pair + v) for v in range(2)]
+            for v in range(2):
+                span, top, total, mix = made[v]
+                if final:
+                    out = (mix * (1.0 / jnp.sum(total, axis=1, keepdims=True))).astype(res.dtype)
+                    for u in range(2):
+                        res[first + 4 * pair + 2 * v + u] = out[u * rows:(u + 1) * rows]
+                else:
+                    m_ref[span, :] = top
+                    l_ref[span, :] = total
+                    acc_ref[span, :] = mix
             return 0
 
-        lax.fori_loop(0, group // 2, step, 0)
+        lax.fori_loop(0, group // 4, step, 0)
 
     def arrive(js):
         for j in js:

time: 93.4 us -> 91.6 us (0.981)
  Pallas kernels: 91.3 us -> 89.5 us
    pallas_call x1, Pallas kernels: 88 us -> 86.2 us  [per_device(): pl.pallas_call(functools.partial(kernel, n, heads), out_shape=(jax.ShapeD...]
where the time goes in v4:
time: 91.6 us; the launch traced here: 91.3 us
  Pallas kernels  89.5 us (98%)
  local copies, waits for them, and re-layouts  0.93 us (1%)
  other arithmetic  0.93 us (1%)
    pallas_call x1, Pallas kernels, per_device(): pl.pallas_call(functools.partial(kernel, n, heads), out_shape=(jax.ShapeD...  86.2 us
    pallas_call x1, Pallas kernels, per_device(): pl.pallas_call(place_kernel, out_shape=jax.ShapeDtypeStruct((members, row...  3.24 us

profile of v4, /device:TPU:1, one launch (start us, length us, event | category | flops | bytes accessed | tf_op | source)
XLA Modules:
  0.0 91.3 jit_solution(3547569564496525092)
XLA Ops:
  0.0 0.9 %pad_bitcast_fusion.1 = (bf16[16,1,16,576]{3,2,1,0:T(8,128)(2,1)S(1)}, bf16[16,1,16,576]{3,2,1,0:T(8,128)(2,1)S(1)}) fusion(bf16[16,2,576]{2,1,0:T(2,128)(2,1)} %param.18), kind=kLoop, calls=%fused_computation.2 | loop fusion | bytes 626688 | tf_op jit(solution)/shard_map/stack | solution.py:334
  0.9 0.9 %pad_maximum_fusion.nk_hbm = bf16[16,2,16,576]{3,2,1,0:T(8,128)(2,1)} fusion(bf16[16,1,16,576]{3,2,1,0:T(8,128)(2,1)S(1)} %get-tuple-element.10, bf16[16,1,16,576]{3,2,1,0:T(8,128)(2,1)S(1)} %get-tuple-element.9), kind=kLoop, calls=%fused_computation | loop fusion | flops 294912 | bytes 1179648 | tf_op jit(solution)/shard_map/stack | solution.py:334
  1.9 86.2 %shard_map.91 = (bf16[25,128,512]{2,1,0:T(8,128)(2,1)}, s32[16]{0:T(128)}) custom-call(s32[16]{0:T(128)} %slot_s.1, s32[16]{0:T(128)} %prompt_s.1, s32[16]{0:T(128)} %length_s.1, s32[1,16]{1,0:T(1,128)} %bitcast.12, bf16[16,128,576]{2,1,0:T(8,128)(2,1)} %bitcast.9, bf16[16,2,16,576]{3,2,1,0:T(8,128)(2,1)} %pad_maximum_fusion.nk_hbm, ...), custom_call_target="tpu_custom_call" | custom-call | tf_op jit(solution)/shard_map/pallas_call | solution.py:342
  88.1 3.2 %shard_map.92 = bf16[16,128,512]{2,1,0:T(8,128)(2,1)} custom-call(s32[16]{0:T(128)} %get-tuple-element.7.src_s, bf16[25,128,512]{2,1,0:T(8,128)(2,1)} %get-tuple-element.8.all_hbm), custom_call_target="tpu_custom_call" | custom-call | tf_op jit(solution)/shard_map/pallas_call | solution.py:396
